TPU v7x, 128 devices: a whole 4x4x4 slice. The times are simulated.
128 devices in a mesh: seq: 32 (over z, y, core), sub: 4 (over x).
Axes of the slice: x: 4, y: 4, z: 4, core: 2. Of those that a mesh axis runs over, the one named last changes fastest.
Arguments:
- queries: bfloat16 [512, 8192], P(('seq', 'sub')), may hold values from -32 to 32, as said below
- query_positions: int32 [512], P(('seq', 'sub')), may hold values from 3584 to 4095
- keys: bfloat16 [524288, 512], P(('seq', 'sub')), may hold values from -8 to 8, as said below
- cache_values: bfloat16 [524288, 512], P(('seq', 'sub')), may hold values from -6 to 6
- cache_length: int32 [1], replicated, may hold values from 262145 to 524288
Outputs:
- scores: float32 [4, 524288], P(None, ('seq', 'sub'))
Inputs may be any that keep to these rules, and one draw needn't show every extreme that they name: `queries`: custom draw; entries bounded. `keys`: custom draw; entries bounded.
All inputs are finite; a program needn't handle non-finite values.
Results may differ from a plain program's by a relative error of at most 0.00077.
Values sent between devices are 32-bit elements; how exact they have to be, the bound alone decides.
No kernel may reach another device: no remote copies, remote signals or barrier semaphores. Data moves between devices by JAX's collectives and lax.ppermute only.
A program may use at most 128 MiB of HBM per device.

v0:
```python
import math

import jax
import jax.numpy as jnp
from jax import lax
from jax.sharding import PartitionSpec as P

H = 64
KVH = 4
HD = 128
QN = 512


def rotate_rows(queries, positions, heads, width):
    count = queries.shape[0]
    values = queries.astype(jnp.float32).reshape(count, heads, width)
    half = width // 2
    freqs = jnp.exp(-jnp.arange(half, dtype=jnp.float32) * (2.0 * math.log(1000000.0) / width))
    angle = positions.astype(jnp.float32)[:, None] * freqs[None, :]
    cosine = jnp.concatenate([jnp.cos(angle), jnp.cos(angle)], axis=1)[:, None, :]
    sine = jnp.concatenate([jnp.sin(angle), jnp.sin(angle)], axis=1)[:, None, :]
    turned = jnp.concatenate([-values[:, :, half:], values[:, :, :half]], axis=2)
    return values * cosine + turned * sine


def local(queries, query_positions, keys, cache_values, cache_length):
    heads, kv_heads, width, group = (H, KVH, HD, H // KVH)
    local_rows = keys.shape[0]
    rotated = rotate_rows(queries, query_positions, heads, width)
    first_sum = jnp.sum(rotated, axis=0)
    outer_sum = jnp.einsum("ihd,ihe->hde", rotated, rotated, precision=lax.Precision.HIGHEST)
    first_sum, outer_sum = lax.psum((first_sum, outer_sum), ("seq", "sub"))
    mean = first_sum / QN
    sigma = (outer_sum / QN - mean[:, :, None] * mean[:, None, :]).astype(jnp.bfloat16)
    sigma_cat = (
        sigma.reshape(kv_heads, group, width, width)
        .transpose(0, 2, 1, 3)
        .reshape(kv_heads, width, group * width)
    )
    mean_groups = mean.reshape(kv_heads, group, width)

    def block_logits(block):
        pieces = []
        for grp in range(kv_heads):
            keyblk = block[:, grp * width : (grp + 1) * width]
            mixed = jnp.dot(keyblk, sigma_cat[grp], preferred_element_type=jnp.float32)
            mixed = mixed.reshape(block.shape[0], group, width)
            inner = mean_groups[grp][None] + mixed * (0.5 / math.sqrt(width))
            keyf = keyblk.astype(jnp.float32)
            pieces.append(jnp.sum(keyf[:, None, :] * inner, axis=2).T / math.sqrt(width))
        return jnp.concatenate(pieces, axis=0)

    block_rows = math.gcd(local_rows, 2048)
    blocks = keys.reshape(local_rows // block_rows, block_rows, kv_heads * width)
    logit = lax.map(block_logits, blocks).transpose(1, 0, 2).reshape(heads, local_rows)
    start = lax.axis_index(("seq", "sub")) * local_rows
    live = (start + jnp.arange(local_rows, dtype=jnp.int32) < cache_length[0])[None, :]
    local_peak = jnp.max(jnp.where(live, logit, jnp.float32(-1e30)), axis=1)
    peak = lax.pmax(local_peak, ("seq", "sub"))
    weights = jnp.where(live, jnp.exp(jnp.where(live, logit - peak[:, None], 0.0)), 0.0)
    total = lax.psum(jnp.sum(weights, axis=1), ("seq", "sub"))
    prob = weights / total[:, None]
    vals = cache_values.reshape(local_rows, kv_heads, width).astype(jnp.float32)
    vnorm = jnp.sqrt(jnp.mean(vals * vals, axis=2)).T
    summed = jnp.sum(prob.reshape(kv_heads, group, local_rows), axis=1)
    everywhere = local_rows * lax.axis_size(("seq", "sub"))
    return summed * (everywhere / group) * vnorm


def solution(mesh):
    return jax.shard_map(
        local,
        mesh=mesh,
        in_specs=(
            P(("seq", "sub"), None),
            P(("seq", "sub")),
            P(("seq", "sub"), None),
            P(("seq", "sub"), None),
            P(),
        ),
        out_specs=P(None, ("seq", "sub")),
        check_vma=False,
    )
```

profile of v0, /device:TPU:1, one launch (start us, length us, event | category | flops | bytes accessed | tf_op | source)
XLA Modules:
  0.0 390.5 jit_solution(4624743822707272962)
XLA Ops:
  8.4 9.7 %fusion.12 = f32[64,128,128]{2,1,0:T(8,128)} fusion(f32[4,128]{1,0:T(4,128)S(1)} %get-tuple-element.63, f32[4,64,64]{2,0,1:T(4,128)S(1)} %get-tuple-element.60, f32[4,64,64]{2,0,1:T(4,128)S(1)} %get-tuple-element.59, f32[4,128]{1,0:T(4,128)S(1)} %get-tuple-element.64, bf16[4,8192]{1,0:T(4,128)(2,1)} %param.7), kind=kOutput, calls=%fused_computation.40 | convolution fusion | flops 50495488 | bytes 4395008 | tf_op jit(solution)/shard_map/ihd,ihe->hde/dot_general | solution.py:31
  18.1 6.6 %convert_multiply_fusion = f32[4096,512]{1,0:T(8,128)} fusion(bf16[4096,512]{1,0:T(8,128)(2,1)} %param.10), kind=kLoop, calls=%fused_computation.27 | loop fusion | flops 4194304 | bytes 12582912 | tf_op jit(solution)/shard_map/mul | solution.py:64
  24.8 10.0 %mul.146 = f32[4096,4,128]{2,1,0:T(4,128)} reshape(f32[4096,512]{1,0:T(8,128)} %convert_multiply_fusion) | data formatting | bytes 16777216 | tf_op jit(solution)/shard_map/mul | solution.py:64
  34.7 9.8 %reduce_sum.78 = f32[4096,4]{1,0:T(8,128)} reduce(f32[4096,4,128]{2,1,0:T(4,128)} %mul.146, f32[]{:T(128)} %constant.47.clone.1), dimensions={2}, to_apply=%region_14.15 | reduce | flops 2080768 | bytes 8454148 | tf_op jit(solution)/shard_map/reduce_sum | solution.py:64
  44.6 2.2 multiply_sqrt_fusion
  48.8 69.6 %psum.21 = f32[64,128]{1,0:T(8,128)S(1)} all-reduce(f32[64,128]{1,0:T(8,128)S(1)} %bitcast.126), channel_id=1, replica_groups=mesh['seq'=32,'sub'=4] {'seq','sub'}, use_global_device_ids=true, to_apply=%region_2.0 | all-reduce | flops 8192 | bytes 65536 | tf_op jit(solution)/shard_map/psum | solution.py:32
  120.3 55.3 %all-reduce.2.cloned.1.call-done = f32[64,128,128]{2,1,0:T(8,128)} async-done(((f32[64,128,128]{2,1,0:T(8,128)}), f32[64,128,128]{2,1,0:T(8,128)}) %all-reduce.2.cloned.1.call-update) | async-done | bytes 4194320 | tf_op jit(solution)/shard_map/psum | solution.py:32
  175.6 3.2 subtract_convert_fusion
  178.8 2.6 copy.48
  181.4 67.0 %while.10 = (s32[]{:T(128)}, f32[2,64,2048]{2,1,0:T(8,128)}, bf16[2,2048,512]{2,1,0:T(8,128)(2,1)}, f32[4,16,128]{2,1,0:T(8,128)}, bf16[4,128,2048]{1,2,0:T(8,128)(2,1)}, /*index=5*/s32[]{:T(128)}) while((s32[]{:T(128)}, f32[2,64,2048]{2,1,0:T(8,128)}, bf16[2,2048,512]{2,1,0:T(8,128)(2,1)}, f32[4,16,128]{2,1,0:T(8,128)}, ...), condition=%wide.region_8.9_spmd, body=%wide.region_3.8_spmd.sunk | while | flops 4363517952 | bytes 46760104 | solution.py:55
  182.2 1.7 dynamic-slice_bitcast_fusion.2
  183.9 1.8 slice_convert_fusion.5
  185.7 2.5 copy.56
  188.2 2.8 fusion.40
  191.1 3.5 multiply_reduce_fusion.8
  194.6 2.5 copy.57
  197.1 4.2 %multiply_reduce_fusion.9 = f32[2048,16]{0,1:T(8,128)S(1)} fusion(f32[16,128]{1,0:T(8,128)S(1)} %get-tuple-element.115, f32[2048,128]{0,1:T(8,128)} %copy.57, bf16[16,128,128]{2,1,0:T(8,128)(2,1)} %bitcast.122, bf16[2048,512]{1,0:T(8,128)(2,1)S(1)} %dynamic-slice_bitcast_fusion.2), kind=kOutput, calls=%fused_computation.1.clone.1 | convolution fusion | flops 1090486272 | bytes 2236416 | tf_op jit(solution)/shard_map/while/body/eval_jaxpr/dot_general | solution.py:46
  201.4 2.5 copy.58
  203.9 4.2 %multiply_reduce_fusion.10 = f32[2048,16]{0,1:T(8,128)S(1)} fusion(f32[16,128]{1,0:T(8,128)S(1)} %get-tuple-element.120, f32[2048,128]{0,1:T(8,128)} %copy.58, bf16[16,128,128]{2,1,0:T(8,128)(2,1)} %bitcast.121, bf16[2048,512]{1,0:T(8,128)(2,1)S(1)} %dynamic-slice_bitcast_fusion.2), kind=kOutput, calls=%fused_computation.2.clone.1 | convolution fusion | flops 1090486272 | bytes 2236416 | tf_op jit(solution)/shard_map/while/body/eval_jaxpr/dot_general | solution.py:46
  209.5 4.3 %multiply_reduce_fusion.11 = f32[2048,16]{0,1:T(8,128)S(1)} fusion(f32[16,128]{1,0:T(8,128)S(1)} %get-tuple-element.123, f32[2048,128]{0,1:T(8,128)} %copy.59, bf16[16,128,128]{2,1,0:T(8,128)(2,1)} %bitcast.120, bf16[2048,512]{1,0:T(8,128)(2,1)S(1)} %dynamic-slice_bitcast_fusion.2), kind=kOutput, calls=%fused_computation.3.clone.1 | convolution fusion | flops 1090486272 | bytes 2236416 | tf_op jit(solution)/shard_map/while/body/eval_jaxpr/dot_general | solution.py:46
  217.4 1.8 slice_convert_fusion.5
  219.2 2.5 copy.56
  221.8 2.8 fusion.40
  224.6 3.5 multiply_reduce_fusion.8
  228.1 2.5 copy.57
  230.6 4.2 %multiply_reduce_fusion.9 = f32[2048,16]{0,1:T(8,128)S(1)} fusion(f32[16,128]{1,0:T(8,128)S(1)} %get-tuple-element.115, f32[2048,128]{0,1:T(8,128)} %copy.57, bf16[16,128,128]{2,1,0:T(8,128)(2,1)} %bitcast.122, bf16[2048,512]{1,0:T(8,128)(2,1)S(1)} %dynamic-slice_bitcast_fusion.2), kind=kOutput, calls=%fused_computation.1.clone.1 | convolution fusion | flops 1090486272 | bytes 2236416 | tf_op jit(solution)/shard_map/while/body/eval_jaxpr/dot_general | solution.py:46
  234.9 2.5 copy.58
  237.5 4.2 %multiply_reduce_fusion.10 = f32[2048,16]{0,1:T(8,128)S(1)} fusion(f32[16,128]{1,0:T(8,128)S(1)} %get-tuple-element.120, f32[2048,128]{0,1:T(8,128)} %copy.58, bf16[16,128,128]{2,1,0:T(8,128)(2,1)} %bitcast.121, bf16[2048,512]{1,0:T(8,128)(2,1)S(1)} %dynamic-slice_bitcast_fusion.2), kind=kOutput, calls=%fused_computation.2.clone.1 | convolution fusion | flops 1090486272 | bytes 2236416 | tf_op jit(solution)/shard_map/while/body/eval_jaxpr/dot_general | solution.py:46
  243.0 4.3 %multiply_reduce_fusion.11 = f32[2048,16]{0,1:T(8,128)S(1)} fusion(f32[16,128]{1,0:T(8,128)S(1)} %get-tuple-element.123, f32[2048,128]{0,1:T(8,128)} %copy.59, bf16[16,128,128]{2,1,0:T(8,128)(2,1)} %bitcast.120, bf16[2048,512]{1,0:T(8,128)(2,1)S(1)} %dynamic-slice_bitcast_fusion.2), kind=kOutput, calls=%fused_computation.3.clone.1 | convolution fusion | flops 1090486272 | bytes 2236416 | tf_op jit(solution)/shard_map/while/body/eval_jaxpr/dot_general | solution.py:46
  250.0 64.2 %pmax.7 = f32[64]{0:T(128)S(1)} all-reduce(f32[64]{0:T(128)S(1)} %select_reduce_fusion.1), channel_id=1, replica_groups=mesh['seq'=32,'sub'=4] {'seq','sub'}, use_global_device_ids=true, to_apply=%region_10.11 | all-reduce | flops 64 | bytes 512 | tf_op jit(solution)/shard_map/pmax | solution.py:59
  315.8 2.0 copy.49
  318.9 63.7 %psum.23 = f32[4,16]{1,0:T(4,128)S(1)} all-reduce(f32[4,16]{1,0:T(4,128)S(1)} %div.53), channel_id=1, replica_groups=mesh['seq'=32,'sub'=4] {'seq','sub'}, use_global_device_ids=true, to_apply=%region_12.13 | all-reduce | flops 64 | bytes 512 | tf_op jit(solution)/shard_map/psum | solution.py:61
  (50 shorter events, 18.5 us)
Async XLA Ops:
  6.5 169.1 %all-reduce.2.cloned.1.call-start = ((), (), s32[]{:S(2)}) async-start(), calls=%async_computation | async-start | bytes 8388608 | tf_op jit(solution)/shard_map/psum | solution.py:32
  44.6 4.1 %copy-start.3 = (bf16[4,8192]{1,0:T(4,128)(2,1)S(1)}, bf16[4,8192]{1,0:T(4,128)(2,1)}, u32[]{:S(2)}) copy-start(bf16[4,8192]{1,0:T(4,128)(2,1)} %param.7) | copy-start | bytes 196612
  188.2 2.8 copy-start
  209.5 4.4 %copy-start.1 = (f32[2,64,2048]{2,1,0:T(8,128)S(1)}, f32[2,64,2048]{2,1,0:T(8,128)}, u32[]{:S(2)}) copy-start(f32[2,64,2048]{2,1,0:T(8,128)} %get-tuple-element.135) | copy-start | bytes 3145732 | tf_op jit(solution)/shard_map/while
  213.9 1.1 copy-start.2
  221.8 2.8 copy-start
  243.0 4.4 %copy-start.1 = (f32[2,64,2048]{2,1,0:T(8,128)S(1)}, f32[2,64,2048]{2,1,0:T(8,128)}, u32[]{:S(2)}) copy-start(f32[2,64,2048]{2,1,0:T(8,128)} %get-tuple-element.135) | copy-start | bytes 3145732 | tf_op jit(solution)/shard_map/while
  247.4 1.1 copy-start.2
  248.5 134.1 %copy-start.5 = (pred[4096]{0:T(1024)(128)(4,1)S(1)}, pred[4096]{0:T(1024)(128)(4,1)}, u32[]{:S(2)}) copy-start(pred[4096]{0:T(1024)(128)(4,1)} %add_compare_fusion.1) | copy-start | bytes 12292
  248.5 134.5 %copy-start.4 = (f32[4096,4]{0,1:T(4,128)S(1)}, f32[4096,4]{0,1:T(4,128)}, u32[]{:S(2)}) copy-start(f32[4096,4]{0,1:T(4,128)} %copy.51) | copy-start | bytes 196612
Sparse Core Ops, SparseCore 0:
  18.3 157.2 all-reduce.1
where the time goes:
time: 392 us; the launch traced here: 391 us
  blocking collectives  197 us (50%)
  waiting for transfers between devices  55.4 us (14%)
  local copies, waits for them, and re-layouts  47.6 us (12%)
  matrix products  42.3 us (11%)
  other arithmetic  33.6 us (9%)
  between operations  14.1 us (4%)
    psum x1, blocking collectives, local(): first_sum, outer_sum = lax.psum((first_sum, outer_sum), ('seq', 'sub'))  69.6 us
    pmax x1, blocking collectives, local(): peak = lax.pmax(local_peak, ('seq', 'sub'))  64.2 us
    psum x1, blocking collectives, local(): total = lax.psum(jnp.sum(weights, axis=1), ('seq', 'sub'))  63.7 us
    psum x1, waiting for transfers between devices, local(): first_sum, outer_sum = lax.psum((first_sum, outer_sum), ('seq', 'sub'))  55.3 us
    dot_general x8, matrix products, block_logits(): mixed = jnp.dot(keyblk, sigma_cat[grp], preferred_element_type=jnp.float32)  32.5 us
    convert_element_type x8, local copies, waits for them, and re-layouts, block_logits(): keyf = keyblk.astype(jnp.float32)  17.9 us
    mul x1, local copies, waits for them, and re-layouts, local(): vnorm = jnp.sqrt(jnp.mean(vals * vals, axis=2)).T  9.97 us
    reduce_sum x1, other arithmetic, local(): vnorm = jnp.sqrt(jnp.mean(vals * vals, axis=2)).T  9.85 us
  transfers between devices with their start and end apart: 1, of which 1 were waited for; matrix products, arithmetic and copies ran while one was open for 8% of the time, Pallas kernels for 0%

commit v1 on v0

v1 whole, which is shorter than its diff:
```python
import math

import jax
import jax.numpy as jnp
from jax import lax
from jax.experimental import pallas as pl
from jax.experimental.pallas import tpu as pltpu
from jax.sharding import Mesh
from jax.sharding import PartitionSpec as P

H = 64
KVH = 4
HD = 128
QN = 512
GROUP = H // KVH
HALF = HD // 2
AXES = ("z", "y", "c", "x")
NZ, NY, NC, NX = 4, 4, 2, 4
OWNERS = NZ * NY
PLANES = OWNERS * NC
HP = H // PLANES
PACK = HALF + 8
OWN_HEADS = H // NC
OWN_GROUPS = KVH // NC
F32 = jnp.float32
BF16 = jnp.bfloat16
VMEM_LIMIT = 56 * 2**20


def iota(shape, dim):
    return lax.broadcasted_iota(jnp.int32, shape, dim)


def rotate_kernel(q_ref, cos_ref, sin_ref, out_ref):
    cos, sin = cos_ref[...], sin_ref[...]
    for plane in range(PLANES):
        zy, core = divmod(plane, NC)
        head = core * OWN_HEADS + zy * HP
        rows = [q_ref[:, (head + i) * HD : (head + i + 1) * HD].astype(F32) for i in range(HP)]
        v = jnp.concatenate(rows, axis=0)
        r = v * cos + pltpu.roll(v, HALF, 1) * sin
        for x in range(NX):
            out_ref[plane * NX + x] = r


def stats_kernel(r_ref, out_ref):
    per = r_ref.shape[1] // HP
    rows = r_ref.shape[0] * r_ref.shape[1]
    x = r_ref[...].reshape(rows, HD)
    sub = lax.rem(iota((rows, HD), 0), r_ref.shape[1]) // per
    row_h, lane_h = iota((HALF, HD), 0), iota((HALF, HD), 1)
    eye = iota((HD, HD), 0) == iota((HD, HD), 1)
    for i in range(HP):
        xi = jnp.where(sub == i, x, 0.0)
        second = lax.dot_general(
            xi, x, (((0,), (0,)), ((), ())), precision=lax.Precision.HIGHEST, preferred_element_type=F32
        )
        mean = jnp.sum(xi, axis=0, keepdims=True) * (1.0 / QN)
        mean_col = jnp.sum(jnp.where(eye, mean, 0.0), axis=1, keepdims=True)
        sigma = second * (1.0 / QN) - mean_col * mean
        diag = jnp.sum(jnp.where(eye, sigma, 0.0), axis=0, keepdims=True)
        packed = jnp.where(row_h < lane_h, sigma[:HALF], pltpu.roll(sigma[HALF:], HALF, 1))
        tail = jnp.concatenate([mean, diag, jnp.zeros((6, HD), F32)], axis=0)
        for o in range(OWNERS):
            out_ref[o, i * PACK : i * PACK + HALF, :] = packed
            out_ref[o, i * PACK + HALF : (i + 1) * PACK, :] = tail


def prep_kernel(k_ref, v_ref, kt_ref, vn_ref):
    kt_ref[...] = k_ref[...].T
    ones = jnp.ones((8, HD), BF16)
    nt = (((1,), (1,)), ((), ()))
    for g in range(KVH):
        v = v_ref[:, g * HD : (g + 1) * HD].astype(F32)
        sq = v * v
        hi = sq.astype(BF16)
        lo = (sq - hi.astype(F32)).astype(BF16)
        s = lax.dot_general(ones, hi, nt, preferred_element_type=F32)
        s = s + lax.dot_general(ones, lo, nt, preferred_element_type=F32)
        vn_ref[g : g + 1, :] = jnp.sqrt(s[:1] * (1.0 / HD))


def unpack(p_ref, w_ref, mu_ref):
    row, lane = iota((HALF, HD), 0), iota((HALF, HD), 1)
    means = []
    for h in range(GROUP):
        o, i = divmod(h, HP)
        packed = p_ref[o, i * PACK : i * PACK + HALF, :]
        tail = p_ref[o, i * PACK + HALF : (i + 1) * PACK, :]
        diag = tail[1:2]
        means.append(tail[0:1])
        top = jnp.where(row < lane, 2.0 * packed, jnp.where(row == lane, diag, 0.0))
        turned = pltpu.roll(packed, HALF, 1)
        down = lane - HALF
        low = jnp.where(down < row, 2.0 * turned, jnp.where(down == row, diag, 0.0))
        low = jnp.where(down >= 0, low, 0.0)
        w_ref[h * HD : h * HD + HALF, :] = top.astype(BF16)
        w_ref[h * HD + HALF : (h + 1) * HD, :] = low.astype(BF16)
    mean = jnp.concatenate(means, axis=0)
    m1 = mean.astype(BF16)
    rest = mean - m1.astype(F32)
    m2 = rest.astype(BF16)
    m3 = (rest - m2.astype(F32)).astype(BF16)
    mu_ref[0:GROUP, :] = m1
    mu_ref[GROUP : 2 * GROUP, :] = m2
    mu_ref[2 * GROUP :, :] = m3


def logits_kernel(copies, sc_ref, p_ref, kt_ref, prev_ref, w_out, st_out, w_ref, mu_ref, kf_ref, lg_ref):
    g, t = pl.program_id(0), pl.program_id(1)
    tile = kt_ref.shape[1]
    step = 256

    @pl.when(t == 0)
    def _():
        unpack(p_ref, w_ref, mu_ref)

    kf_ref[...] = kt_ref[...].astype(F32)
    rows = pl.ds(pl.multiple_of(g * GROUP, GROUP), GROUP)
    for s in range(0, tile, step):
        kt = kt_ref[:, s : s + step]
        kf = kf_ref[:, s : s + step]
        lin = jnp.dot(mu_ref[...], kt, preferred_element_type=F32)
        lin = (lin[:GROUP] + lin[GROUP : 2 * GROUP]) + lin[2 * GROUP :]
        quad = []
        for h in range(GROUP):
            m = jnp.dot(w_ref[h * HD : (h + 1) * HD, :], kt, preferred_element_type=F32)
            quad.append(jnp.sum(m * kf, axis=0, keepdims=True))
        quad = jnp.concatenate(quad, axis=0)
        cols = pl.ds(pl.multiple_of(t * tile + s, step), step)
        lg_ref[rows, cols] = quad * (0.5 / HD) + lin * (1.0 / math.sqrt(HD))

    @pl.when((g == pl.num_programs(0) - 1) & (t == pl.num_programs(1) - 1))
    def _():
        heads, width = lg_ref.shape
        lg = lg_ref[...]
        live = sc_ref[1] + iota((heads, width), 1) < sc_ref[2]
        peak = jnp.max(jnp.where(live, lg, -1e30), axis=1, keepdims=True)
        w = jnp.where(live, jnp.exp(jnp.where(live, lg - peak, 0.0)), 0.0)
        w_out[...] = w
        total = jnp.sum(w, axis=1, keepdims=True)
        at = sc_ref[0] * GROUP + iota((heads, 2 * H), 0)
        lane = iota((heads, 2 * H), 1)
        both = jnp.where(lane == at, peak, 0.0) + jnp.where(lane == at + H, total, 0.0)
        st = jnp.sum(both, axis=0, keepdims=True) + prev_ref[0:1, :]
        st_out[...] = jnp.broadcast_to(st, (copies, 2 * H))


def scores_kernel(sc_ref, all_ref, mine_ref, wa_ref, wb_ref, vn_ref, out_ref, ca_ref, cb_ref):
    @pl.when(pl.program_id(0) == 0)
    def _():
        every = all_ref[...]
        lane = iota((1, 2 * H), 1)
        peaks = every
        peak = jnp.max(peaks, axis=0, keepdims=True)
        sums = pltpu.roll(every, H, 1)
        valid = iota(every.shape, 1) < H
        total = jnp.sum(jnp.where(valid, jnp.exp(jnp.where(valid, peaks - peak, 0.0)) * sums, 0.0), axis=0, keepdims=True)
        ok = lane < H
        mine = mine_ref[0:1, :]
        scale = jnp.where(ok, jnp.exp(jnp.where(ok, mine - peak, 0.0)) / jnp.where(ok, total, 1.0), 0.0)
        shape = (OWN_HEADS, 2 * H)
        for ref, first in ((ca_ref, sc_ref[0] * GROUP), (cb_ref, (OWN_GROUPS - sc_ref[0]) * GROUP)):
            pick = iota(shape, 1) == first + iota(shape, 0)
            ref[...] = jnp.broadcast_to(jnp.sum(jnp.where(pick, scale, 0.0), axis=1, keepdims=True), ref.shape)

    width = out_ref.shape[1]

    def sums_of(w_ref, c_ref):
        w = w_ref[...] * c_ref[:, 0:1]
        return jnp.sum(w.reshape(OWN_GROUPS, GROUP, width), axis=1)

    a, b = sums_of(wa_ref, ca_ref), sums_of(wb_ref, cb_ref)
    first = sc_ref[0] == 0
    low, high = jnp.where(first, a, b), jnp.where(first, b, a)
    positions = sc_ref[3].astype(F32)
    out_ref[...] = jnp.concatenate([low, high], axis=0) * (positions / GROUP) * vn_ref[...]


def params(**kw):
    return pltpu.CompilerParams(vmem_limit_bytes=VMEM_LIMIT, **kw)


def local(queries, query_positions, keys, cache_values, cache_length):
    devices = NZ * NY * NC * NX
    n = keys.shape[0]
    nq = queries.shape[0]
    freqs = jnp.exp(-jnp.arange(HALF, dtype=F32) * (2.0 * math.log(1000000.0) / HD))
    angle = query_positions.astype(F32)[:, None] * freqs[None, :]
    cosine, sine = jnp.cos(angle), jnp.sin(angle)
    cosine = jnp.tile(jnp.concatenate([cosine, cosine], axis=1), (HP, 1))
    sine = jnp.tile(jnp.concatenate([-sine, sine], axis=1), (HP, 1))
    sent = pl.pallas_call(
        rotate_kernel,
        out_shape=jax.ShapeDtypeStruct((devices, HP * nq, HD), F32),
        compiler_params=params(),
        name="rotate",
    )(queries, cosine, sine)
    rotated = lax.all_to_all(sent, AXES, 0, 0)

    block = 512
    kt, vnorm = pl.pallas_call(
        prep_kernel,
        grid=(n // block,),
        in_specs=[pl.BlockSpec((block, KVH * HD), lambda i: (i, 0))] * 2,
        out_specs=[pl.BlockSpec((KVH * HD, block), lambda i: (0, i)), pl.BlockSpec((KVH, block), lambda i: (0, i))],
        out_shape=[jax.ShapeDtypeStruct((KVH * HD, n), BF16), jax.ShapeDtypeStruct((KVH, n), F32)],
        compiler_params=params(),
        cost_estimate=pl.CostEstimate(flops=2 * n * 512 * 32, bytes_accessed=12 * 2**20, transcendentals=0),
        name="prep",
    )(keys, cache_values)

    packed = pl.pallas_call(
        stats_kernel,
        out_shape=jax.ShapeDtypeStruct((OWNERS, HP * PACK, HD), F32),
        compiler_params=params(),
        name="stats",
    )(rotated)
    mine = lax.all_to_all(packed, ("z", "y"), 0, 0)
    other = lax.ppermute(mine, "c", [(0, 1), (1, 0)])

    core = lax.axis_index("c")
    start = lax.axis_index(AXES) * n
    everywhere = n * devices

    def scalars(which):
        return jnp.stack([which * OWN_GROUPS, start, cache_length[0], jnp.int32(everywhere)]).astype(jnp.int32)

    tile = 2048
    groups = OWNERS * HP // GROUP
    owners = OWNERS // groups

    def logits(which, stats, prev, copies, name):
        return pl.pallas_call(
            lambda *refs: logits_kernel(copies, *refs),
            grid_spec=pltpu.PrefetchScalarGridSpec(
                num_scalar_prefetch=1,
                grid=(groups, n // tile),
                in_specs=[
                    pl.BlockSpec((owners, HP * PACK, HD), lambda g, t, sc: (g, 0, 0)),
                    pl.BlockSpec((HD, tile), lambda g, t, sc: (sc[0] + g, t)),
                    pl.BlockSpec((8, 2 * H), lambda g, t, sc: (0, 0)),
                ],
                out_specs=[
                    pl.BlockSpec((OWN_HEADS, n), lambda g, t, sc: (0, 0)),
                    pl.BlockSpec((copies, 2 * H), lambda g, t, sc: (0, 0)),
                ],
                scratch_shapes=[
                    pltpu.VMEM((GROUP * HD, HD), BF16),
                    pltpu.VMEM((3 * GROUP, HD), BF16),
                    pltpu.VMEM((HD, tile), F32),
                    pltpu.VMEM((OWN_HEADS, n), F32),
                ],
            ),
            out_shape=[
                jax.ShapeDtypeStruct((OWN_HEADS, n), F32),
                jax.ShapeDtypeStruct((copies, 2 * H), F32),
            ],
            compiler_params=params(),
            cost_estimate=pl.CostEstimate(
                flops=2 * n * OWN_HEADS * HD * HD, bytes_accessed=4 * 2**20, transcendentals=n * OWN_HEADS
            ),
            name=name,
        )(scalars(which), stats, kt, prev)

    w_mine, st_mine = logits(core, mine, jnp.zeros((8, 2 * H), F32), 8, "logits_own")
    w_other, st = logits(1 - core, other, st_mine, devices, "logits_other")
    every = lax.all_to_all(st, AXES, 0, 0)

    part = n // 2
    return pl.pallas_call(
        scores_kernel,
        grid_spec=pltpu.PrefetchScalarGridSpec(
            num_scalar_prefetch=1,
            grid=(n // part,),
            in_specs=[
                pl.BlockSpec((devices, 2 * H), lambda i, sc: (0, 0)),
                pl.BlockSpec((8, 2 * H), lambda i, sc: (0, 0)),
                pl.BlockSpec((OWN_HEADS, part), lambda i, sc: (0, i)),
                pl.BlockSpec((OWN_HEADS, part), lambda i, sc: (0, i)),
                pl.BlockSpec((KVH, part), lambda i, sc: (0, i)),
            ],
            out_specs=pl.BlockSpec((KVH, part), lambda i, sc: (0, i)),
            scratch_shapes=[pltpu.VMEM((OWN_HEADS, HD), F32)] * 2,
        ),
        out_shape=jax.ShapeDtypeStruct((KVH, n), F32),
        compiler_params=params(),
        name="scores",
    )(scalars(core), every, st, w_mine, w_other, vnorm)


def solution(mesh):
    fine = Mesh(mesh.devices.reshape(NZ, NY, NC, NX), AXES)
    return jax.shard_map(
        local,
        mesh=fine,
        in_specs=(P(AXES, None), P(AXES), P(AXES, None), P(AXES, None), P()),
        out_specs=P(None, AXES),
        check_vma=False,
    )
```

time: 392 us -> 112 us (0.29)
  blocking collectives: 197 us -> 62.1 us
  waiting for transfers between devices: 55.4 us -> 0.01 us
  local copies, waits for them, and re-layouts: 47.6 us -> 2.81 us
  Pallas kernels: 0 us -> 43.4 us
  matrix products: 42.3 us -> 0 us
  other arithmetic: 33.6 us -> 1.53 us
  between operations: 14.1 us -> 0.67 us
    psum x2 -> x0, blocking collectives: 133 us -> none  [the longest x1 69.6 us: local(): first_sum, outer_sum = lax.psum((first_sum, outer_sum), ('seq', 'sub'))]
    pmax x1 -> x0, blocking collectives: 64.2 us -> none  [local(): peak = lax.pmax(local_peak, ('seq', 'sub'))]
    all_to_all x0 -> x3, blocking collectives: none -> 62.1 us  [the longest x1 25.6 us: local(): rotated = lax.all_to_all(sent, AXES, 0, 0)]
    psum x1 -> x0, waiting for transfers between devices: 55.3 us -> none  [local(): first_sum, outer_sum = lax.psum((first_sum, outer_sum), ('seq', 'sub'))]
    pallas_call x0 -> x6, Pallas kernels: none -> 43.4 us  [the longest x2 26.7 us: logits(): pl.pallas_call(lambda *refs: logits_kernel(copies, *refs), grid_spec=pltp...]
    dot_general x9 -> x0, matrix products: 42.3 us -> none  [the longest x8 32.5 us: block_logits(): mixed = jnp.dot(keyblk, sigma_cat[grp], preferred_element_type=jnp.float32)]
    convert_element_type x8 -> x0, local copies, waits for them, and re-layouts: 17.9 us -> none  [block_logits(): keyf = keyblk.astype(jnp.float32)]
    reduce_sum x4 -> x0, other arithmetic: 12.1 us -> none  [the longest x1 9.85 us: local(): vnorm = jnp.sqrt(jnp.mean(vals * vals, axis=2)).T]
  transfers between devices with their start and end apart: 1 -> 1, of which waited for: 1 -> 0; matrix products, arithmetic and copies ran while one was open for 8% -> 1% of each run, Pallas kernels for 0% -> 20%
where the time goes in v1:
time: 112 us
  blocking collectives  62.1 us (55%)
  Pallas kernels  43.4 us (39%)
  local copies, waits for them, and re-layouts  2.81 us (3%)
  other arithmetic  1.53 us (1%)
  starting transfers between devices  1.23 us (1%)
    pallas_call x2, Pallas kernels, logits(): pl.pallas_call(lambda *refs: logits_kernel(copies, *refs), grid_spec=pltp...  26.7 us
    all_to_all x1, blocking collectives, local(): rotated = lax.all_to_all(sent, AXES, 0, 0)  25.6 us
    all_to_all x1, blocking collectives, local(): mine = lax.all_to_all(packed, ('z', 'y'), 0, 0)  22 us
    all_to_all x1, blocking collectives, local(): every = lax.all_to_all(st, AXES, 0, 0)  14.5 us
    pallas_call x1, Pallas kernels, local(): pl.pallas_call(prep_kernel, grid=(n // block,), in_specs=[pl.BlockSpec((b...  8.58 us
    pallas_call x1, Pallas kernels, local(): pl.pallas_call(stats_kernel, out_shape=jax.ShapeDtypeStruct((OWNERS, HP *...  3.39 us
    pallas_call x1, Pallas kernels, local(): pl.pallas_call(scores_kernel, grid_spec=pltpu.PrefetchScalarGridSpec(num_...  2.96 us
  transfers between devices with their start and end apart: 1, of which 0 were waited for; matrix products, arithmetic and copies ran while one was open for 1% of the time, Pallas kernels for 20%

profile of v1, /device:TPU:1, one launch (start us, length us, event | category | flops | bytes accessed | tf_op | source)
XLA Modules:
  0.0 111.7 jit_solution(4039448139845184175)
XLA Ops:
  0.0 0.7 convert_element_type.3
  0.7 0.1 fusion
  0.8 0.1 pad_maximum_fusion
  0.9 0.6 tile.8
  1.5 0.6 tile.20
  2.1 1.8 %rotate.1 = f32[128,8,128]{2,1,0:T(8,128)} custom-call(bf16[4,8192]{1,0:T(4,128)(2,1)} %q_ref.1, f32[8,128]{1,0:T(8,128)} %bitcast.11, f32[8,128]{1,0:T(8,128)} %bitcast.12), custom_call_target="tpu_custom_call" | custom-call | tf_op jit(solution)/shard_map/rotate/pallas_call | solution.py:193
  3.8 25.6 %all_to_all.21.r_ref = f32[128,8,128]{2,1,0:T(8,128)} all-to-all(f32[128,8,128]{2,1,0:T(8,128)} %rotate.1), channel_id=1, replica_groups=mesh['z'=4,'y'=4,'c'=2,'x'=4] {'z','y','c','x'}, dimensions={0} | all-to-all | bytes 1048576 | tf_op jit(solution)/shard_map/all_to_all | solution.py:199
  29.4 3.4 %stats.1 = f32[16,144,128]{2,1,0:T(8,128)} custom-call(f32[128,8,128]{2,1,0:T(8,128)} %all_to_all.21.r_ref), custom_call_target="tpu_custom_call" | custom-call | tf_op jit(solution)/shard_map/stats/pallas_call | solution.py:213
  32.8 22.0 %all_to_all.22.refs_1_ = f32[16,144,128]{2,1,0:T(8,128)S(1)} all-to-all(f32[16,144,128]{2,1,0:T(8,128)} %stats.1), channel_id=1, replica_groups=mesh['z'=4,'y'=4,'c'=2,'x'=4] {'z','y'}, dimensions={0} | all-to-all | bytes 2359296 | tf_op jit(solution)/shard_map/all_to_all | solution.py:219
  54.8 0.0 copy-start
  54.8 1.2 %collective-permute-start = (f32[16,144,128]{2,1,0:T(8,128)S(1)}, f32[16,144,128]{2,1,0:T(8,128)S(1)}, u32[]{:S(2)}, u32[]{:S(2)}) collective-permute-start(f32[16,144,128]{2,1,0:T(8,128)S(1)} %all_to_all.22.refs_1_), channel_id=1, source_target_pairs={{0,4},{4,0},{1,5},{5,1},{2,6},{6,2},{3,7},{7,3},{8,12},{12,8},{9,1... | collective-permute-start | bytes 3538952 | tf_op jit(solution)/shard_map/ppermute | solution.py:220
  56.7 8.6 %prep.1 = (bf16[512,4096]{1,0:T(8,128)(2,1)}, f32[4,4096]{1,0:T(4,128)}) custom-call(bf16[4096,512]{1,0:T(8,128)(2,1)} %k_ref.1, bf16[4096,512]{1,0:T(8,128)(2,1)} %v_ref.1), custom_call_target="tpu_custom_call" | custom-call | flops 134217728 | bytes 12582912 | tf_op jit(solution)/shard_map/prep/pallas_call | solution.py:202
  65.2 0.0 copy-done
  65.2 0.7 pad_add_fusion
  65.9 0.6 broadcast_in_dim.2.refs_3_
  66.5 13.3 %logits_own.1 = (f32[32,4096]{1,0:T(8,128)}, f32[8,128]{1,0:T(8,128)}) custom-call(s32[4]{0:T(128)} %get-tuple-element.21.refs_0_.sc_ref, f32[16,144,128]{2,1,0:T(8,128)} %copy-done, bf16[512,4096]{1,0:T(8,128)(2,1)} %get-tuple-element.11.refs_2_, f32[8,128]{1,0:T(8,128)} %broadcast_in_dim.2.refs_3_), custom_call_target="tpu_custom_call" | custom-call | flops 4294967296 | bytes 4194304 | tf_op jit(solution)/shard_map/logits_own/pallas_call | solution.py:234
  79.8 0.0 collective-permute-done.refs_1_
  79.9 0.0 copy-start.1
  79.9 1.0 copy-done.1
  80.9 13.3 %logits_other.1 = (f32[32,4096]{1,0:T(8,128)}, f32[128,128]{1,0:T(8,128)}) custom-call(s32[4]{0:T(128)} %get-tuple-element.20.refs_0_, f32[16,144,128]{2,1,0:T(8,128)} %copy-done.1, bf16[512,4096]{1,0:T(8,128)(2,1)} %get-tuple-element.11.refs_2_, f32[8,128]{1,0:T(8,128)} %get-tuple-element.12.refs_3_), custom_call_target="tpu_custom_call" | custom-call | flops 4294967296 | bytes 4194304 | tf_op jit(solution)/shard_map/logits_other/pallas_call | solution.py:234
  94.2 14.5 %all_to_all.23 = f32[128,1,128]{2,1,0:T(1,128)} all-to-all(f32[128,1,128]{2,1,0:T(1,128)} %bitcast.9), channel_id=1, replica_groups=mesh['z'=4,'y'=4,'c'=2,'x'=4] {'z','y','c','x'}, dimensions={0} | all-to-all | bytes 131072 | tf_op jit(solution)/shard_map/all_to_all | solution.py:268
  108.8 3.0 %scores.1 = f32[4,4096]{1,0:T(4,128)} custom-call(s32[4]{0:T(128)} %get-tuple-element.21.refs_0_.sc_ref, f32[128,128]{1,0:T(8,128)} %bitcast.10, f32[128,128]{1,0:T(8,128)} %get-tuple-element.13.mine_ref, f32[32,4096]{1,0:T(8,128)} %get-tuple-element.14.wa_ref, f32[32,4096]{1,0:T(8,128)} %get-tuple-element.15.wb_ref, f32[4,4096]{1,0:T(4,128)} %get-tuple-element.16.vn_ref), custom_call_target="tpu_custom_call" | custom-call | tf_op jit(solution)/shard_map/scores/pallas_call | solution.py:271
  (1 shorter events, 0.0 us)
Async XLA Ops:
  54.8 10.5 %copy-start = (f32[16,144,128]{2,1,0:T(8,128)}, f32[16,144,128]{2,1,0:T(8,128)S(1)}, u32[]{:S(2)}) copy-start(f32[16,144,128]{2,1,0:T(8,128)S(1)} %all_to_all.22.refs_1_) | copy-start | bytes 3538948
  54.8 25.1 %collective-permute-start = (f32[16,144,128]{2,1,0:T(8,128)S(1)}, f32[16,144,128]{2,1,0:T(8,128)S(1)}, u32[]{:S(2)}, u32[]{:S(2)}) collective-permute-start(f32[16,144,128]{2,1,0:T(8,128)S(1)} %all_to_all.22.refs_1_), channel_id=1, source_target_pairs={{0,4},{4,0},{1,5},{5,1},{2,6},{6,2},{3,7},{7,3},{8,12},{12,8},{9,1... | collective-permute-start | bytes 3538952 | tf_op jit(solution)/shard_map/ppermute | solution.py:220
  79.9 1.0 copy-start.1

commit v2 on v0

v2 whole, which is shorter than its diff:
```python
import functools
import math

import jax
import jax.numpy as jnp
from jax import lax
from jax.experimental import pallas as pl
from jax.experimental.pallas import tpu as pltpu
from jax.sharding import Mesh
from jax.sharding import PartitionSpec as P

H = 64
KVH = 4
HD = 128
QN = 512
GROUP = H // KVH
HALF = HD // 2
AXES = ("z", "y", "c", "x")
NZ, NY, NC, NX = 4, 4, 2, 4
DEVICES = NZ * NY * NC * NX
OWNERS = NZ * NY
PLANES = OWNERS * NC
HP = H // PLANES
PACK = HP * HALF + 8
OWN_HEADS = H // NC
OWN_GROUPS = KVH // NC
GROUP_OWNERS = OWNERS // OWN_GROUPS
F32 = jnp.float32
BF16 = jnp.bfloat16
VMEM = pl.BlockSpec(memory_space=pltpu.VMEM)
SMEM = pl.BlockSpec(memory_space=pltpu.SMEM)
HBM = pl.BlockSpec(memory_space=pltpu.HBM)


def iota(shape, dim):
    return lax.broadcasted_iota(jnp.int32, shape, dim)


def rotate_kernel(pos_hbm, q_hbm, out_ref, pos_ref, q_ref, sems):
    nq = q_ref.shape[0]
    pos_copy = pltpu.make_async_copy(pos_hbm, pos_ref, sems.at[0])
    q_copy = pltpu.make_async_copy(q_hbm, q_ref, sems.at[1])
    pos_copy.start()
    q_copy.start()
    rows = HP * nq
    query = lax.rem(iota((rows, HD), 0), nq)
    lane = iota((rows, HD), 1)
    position = jnp.zeros((rows, HD), F32)
    pos_copy.wait()
    for i in range(nq):
        position = jnp.where(query == i, pos_ref[i].astype(F32), position)
    freqs = jnp.exp(-lax.rem(lane, HALF).astype(F32) * (2.0 * math.log(1000000.0) / HD))
    angle = position * freqs
    cos, sin = jnp.cos(angle), jnp.sin(angle)
    sin = jnp.where(lane < HALF, -sin, sin)
    q_copy.wait()
    for plane in range(PLANES):
        zy, core = divmod(plane, NC)
        head = core * OWN_HEADS + zy * HP
        v = jnp.concatenate(
            [q_ref[:, (head + i) * HD : (head + i + 1) * HD].astype(F32) for i in range(HP)], axis=0
        )
        r = v * cos + pltpu.roll(v, HALF, 1) * sin
        for x in range(NX):
            out_ref[plane * NX + x] = r


def stats_kernel(r_ref, out_ref):
    half = r_ref.shape[0] // 2
    rows = half * r_ref.shape[1]
    nq = r_ref.shape[1] // HP
    xa = r_ref[:half].reshape(rows, HD)
    xb = r_ref[half:].reshape(rows, HD)
    first = lax.rem(iota((rows, HD), 0), r_ref.shape[1]) < nq
    heads = (
        jnp.where(first, xa, pltpu.roll(xb, nq, 0)),
        jnp.where(first, pltpu.roll(xa, rows - nq, 0), xb),
    )
    row_h, lane_h = iota((HALF, HD), 0), iota((HALF, HD), 1)
    eye = iota((HD, HD), 0) == iota((HD, HD), 1)
    tail = []
    for i, x in enumerate(heads):
        second = lax.dot_general(
            x, x, (((0,), (0,)), ((), ())), precision=lax.Precision.HIGHEST, preferred_element_type=F32
        )
        mean = jnp.sum(x, axis=0, keepdims=True) * (1.0 / QN)
        mean_col = jnp.sum(jnp.where(eye, mean, 0.0), axis=1, keepdims=True)
        sigma = second * (1.0 / QN) - mean_col * mean
        diag = jnp.sum(jnp.where(eye, sigma, 0.0), axis=0, keepdims=True)
        packed = jnp.where(row_h < lane_h, sigma[:HALF], pltpu.roll(sigma[HALF:], HALF, 1))
        for o in range(OWNERS):
            out_ref[o, i * HALF : (i + 1) * HALF, :] = packed
        tail += [mean, diag]
    tail = jnp.concatenate(tail + [jnp.zeros((8 - 2 * HP, HD), F32)], axis=0)
    for o in range(OWNERS):
        out_ref[o, HP * HALF :, :] = tail


def prep_kernel(k_ref, v_ref, own_ref, other_ref, vn_ref):
    wide = OWN_GROUPS * HD
    low, high = k_ref[:, :wide], k_ref[:, wide:]
    first = lax.axis_index("c") == 0
    own_ref[...] = jnp.where(first, low, high).T
    other_ref[...] = jnp.where(first, high, low).T
    ones = jnp.ones((8, HD), BF16)
    nt = (((1,), (1,)), ((), ()))
    for g in range(KVH):
        v = v_ref[:, g * HD : (g + 1) * HD].astype(F32)
        sq = v * v
        hi = sq.astype(BF16)
        lo = (sq - hi.astype(F32)).astype(BF16)
        s = lax.dot_general(ones, hi, nt, preferred_element_type=F32)
        s = s + lax.dot_general(ones, lo, nt, preferred_element_type=F32)
        vn_ref[g : g + 1, :] = jnp.sqrt(s[:1] * (1.0 / HD))


def unpack(p_ref, g, w_ref, mu_ref):
    row, lane = iota((HALF, HD), 0), iota((HALF, HD), 1)
    down = lane - HALF
    means = []
    for h in range(GROUP):
        o, i = divmod(h, HP)
        packed = p_ref[g * GROUP_OWNERS + o, i * HALF : (i + 1) * HALF, :]
        tail = p_ref[g * GROUP_OWNERS + o, HP * HALF :, :]
        diag = tail[2 * i + 1 : 2 * i + 2]
        means.append(tail[2 * i : 2 * i + 1])
        top = jnp.where(row < lane, 2.0 * packed, jnp.where(row == lane, diag, 0.0))
        low = jnp.where(down < row, 2.0 * pltpu.roll(packed, HALF, 1), jnp.where(down == row, diag, 0.0))
        low = jnp.where(down >= 0, low, 0.0)
        w_ref[h * HD : h * HD + HALF, :] = top.astype(BF16)
        w_ref[h * HD + HALF : (h + 1) * HD, :] = low.astype(BF16)
    mean = jnp.concatenate(means, axis=0)
    m1 = mean.astype(BF16)
    rest = mean - m1.astype(F32)
    m2 = rest.astype(BF16)
    m3 = (rest - m2.astype(F32)).astype(BF16)
    mu_ref[0:GROUP, :] = m1
    mu_ref[GROUP : 2 * GROUP, :] = m2
    mu_ref[2 * GROUP :, :] = m3


def logits_kernel(own, len_ref, p_ref, kt_ref, *refs):
    prev_ref, (w_out, st_out, w_ref, mu_ref) = (None, refs) if own else (refs[0], refs[1:])
    core = lax.axis_index("c")
    side = core if own else 1 - core
    width = kt_ref.shape[1]
    step = 256

    def group(g, carry):
        unpack(p_ref, g, w_ref, mu_ref)
        base = pl.multiple_of(g * HD, HD)
        rows = pl.ds(pl.multiple_of(g * GROUP, GROUP), GROUP)
        for s in range(0, width, step):
            kt = kt_ref[pl.ds(base, HD), s : s + step]
            kf = kt.astype(F32)
            lin = jnp.dot(mu_ref[...], kt, preferred_element_type=F32)
            lin = (lin[:GROUP] + lin[GROUP : 2 * GROUP]) + lin[2 * GROUP :]
            quad = []
            for h in range(GROUP):
                m = jnp.dot(w_ref[h * HD : (h + 1) * HD, :], kt, preferred_element_type=F32)
                quad.append(jnp.sum(m * kf, axis=0, keepdims=True))
            quad = jnp.concatenate(quad, axis=0)
            w_out[rows, s : s + step] = quad * (0.5 / HD) + lin * (1.0 / math.sqrt(HD))
        return carry

    lax.fori_loop(0, OWN_GROUPS, group, 0)
    lg = w_out[...]
    live = lax.axis_index(AXES) * width + iota(lg.shape, 1) < len_ref[0]
    peak = jnp.max(jnp.where(live, lg, -1e30), axis=1, keepdims=True)
    w = jnp.where(live, jnp.exp(jnp.where(live, lg - peak, 0.0)), 0.0)
    w_out[...] = w
    total = jnp.sum(w, axis=1, keepdims=True)
    shape = (OWN_HEADS, 2 * H)
    lane, at = iota(shape, 1), side * OWN_HEADS + iota(shape, 0)
    both = jnp.where(lane == at, peak, 0.0) + jnp.where(lane == at + H, total, 0.0)
    st = jnp.sum(both, axis=0, keepdims=True)
    if not own:
        st = st + prev_ref[0:1, :]
    st_out[...] = jnp.broadcast_to(st, st_out.shape)


def scores_kernel(all_ref, mine_ref, wa_ref, wb_ref, vn_ref, out_ref):
    core = lax.axis_index("c")
    every = all_ref[...]
    valid = iota(every.shape, 1) < H
    peak = jnp.max(every, axis=0, keepdims=True)
    sums = pltpu.roll(every, H, 1)
    total = jnp.where(valid, jnp.exp(jnp.where(valid, every - peak, 0.0)) * sums, 0.0)
    total = jnp.sum(total, axis=0, keepdims=True)
    ok = valid[:1]
    mine = jnp.exp(jnp.where(ok, mine_ref[0:1, :] - peak, 0.0))
    scale = jnp.where(ok, mine / jnp.where(ok, total, 1.0), 0.0)
    shape = (OWN_HEADS, 2 * H)
    width = out_ref.shape[1]

    def sums_of(w_ref, side):
        pick = iota(shape, 1) == side * OWN_HEADS + iota(shape, 0)
        column = jnp.sum(jnp.where(pick, scale, 0.0), axis=1, keepdims=True)
        return jnp.sum((w_ref[...] * column).reshape(OWN_GROUPS, GROUP, width), axis=1)

    a, b = sums_of(wa_ref, core), sums_of(wb_ref, 1 - core)
    low, high = jnp.where(core == 0, a, b), jnp.where(core == 0, b, a)
    out_ref[...] = jnp.concatenate([low, high], axis=0) * (width * DEVICES / GROUP) * vn_ref[...]


def params(mib):
    return pltpu.CompilerParams(vmem_limit_bytes=mib * 2**20)


def local(queries, query_positions, keys, cache_values, cache_length):
    n = keys.shape[0]
    nq = queries.shape[0]
    sent = pl.pallas_call(
        rotate_kernel,
        in_specs=[HBM, HBM],
        out_specs=VMEM,
        out_shape=jax.ShapeDtypeStruct((DEVICES, HP * nq, HD), F32),
        scratch_shapes=[
            pltpu.SMEM((nq,), jnp.int32),
            pltpu.VMEM(queries.shape, BF16),
            pltpu.SemaphoreType.DMA((2,)),
        ],
        compiler_params=params(58),
        name="rotate",
    )(query_positions, queries)
    rotated = lax.all_to_all(sent, AXES, 0, 0)

    block = 1024
    half = pl.BlockSpec((OWN_GROUPS * HD, block), lambda i: (0, i))
    half_shape = jax.ShapeDtypeStruct((OWN_GROUPS * HD, n), BF16)
    kt_own, kt_other, vnorm = pl.pallas_call(
        prep_kernel,
        grid=(n // block,),
        in_specs=[pl.BlockSpec((block, KVH * HD), lambda i: (i, 0))] * 2,
        out_specs=[half, half, pl.BlockSpec((KVH, block), lambda i: (0, i))],
        out_shape=[half_shape, half_shape, jax.ShapeDtypeStruct((KVH, n), F32)],
        compiler_params=params(56),
        cost_estimate=pl.CostEstimate(flops=2 * n * 512 * 512, bytes_accessed=12 * 2**20, transcendentals=0),
        name="prep",
    )(keys, cache_values)
    rotated, kt_own, kt_other, vnorm = lax.optimization_barrier((rotated, kt_own, kt_other, vnorm))

    packed = pl.pallas_call(
        stats_kernel,
        in_specs=[VMEM],
        out_specs=VMEM,
        out_shape=jax.ShapeDtypeStruct((OWNERS, PACK, HD), F32),
        compiler_params=params(16),
        name="stats",
    )(rotated)
    mine = lax.all_to_all(packed, ("z", "y"), 0, 0)
    other = lax.ppermute(mine, "c", [(0, 1), (1, 0)])

    def logits(stats, kt, prev, copies):
        own = prev is None
        return pl.pallas_call(
            functools.partial(logits_kernel, own),
            in_specs=[SMEM, VMEM, VMEM] + [VMEM] * (not own),
            out_specs=[VMEM, VMEM],
            out_shape=[
                jax.ShapeDtypeStruct((OWN_HEADS, n), F32),
                jax.ShapeDtypeStruct((copies, 2 * H), F32),
            ],
            scratch_shapes=[pltpu.VMEM((GROUP * HD, HD), BF16), pltpu.VMEM((3 * GROUP, HD), BF16)],
            compiler_params=params(16),
            cost_estimate=pl.CostEstimate(
                flops=2 * n * OWN_HEADS * HD * HD, bytes_accessed=4 * 2**20, transcendentals=n * OWN_HEADS
            ),
            name="logits_own" if own else "logits_other",
        )(cache_length, stats, kt, *(() if own else (prev,)))

    w_mine, st_mine = logits(mine, kt_own, None, 8)
    w_other, st = logits(other, kt_other, st_mine, DEVICES)
    every = lax.all_to_all(st, AXES, 0, 0)

    return pl.pallas_call(
        scores_kernel,
        in_specs=[VMEM] * 5,
        out_specs=VMEM,
        out_shape=jax.ShapeDtypeStruct((KVH, n), F32),
        compiler_params=params(16),
        name="scores",
    )(every, st, w_mine, w_other, vnorm)


def solution(mesh):
    fine = Mesh(mesh.devices.reshape(NZ, NY, NC, NX), AXES)
    return jax.shard_map(
        local,
        mesh=fine,
        in_specs=(P(AXES, None), P(AXES), P(AXES, None), P(AXES, None), P()),
        out_specs=P(None, AXES),
        check_vma=False,
    )
```

time: 392 us -> 84.6 us (0.22)
  blocking collectives: 197 us -> 33 us
  waiting for transfers between devices: 55.4 us -> 7.08 us
  local copies, waits for them, and re-layouts: 47.6 us -> 0.01 us
  matrix products: 42.3 us -> 0 us
  other arithmetic: 33.6 us -> 0 us
  Pallas kernels: 0 us -> 30.1 us
  starting transfers between devices: 0.01 us -> 13.4 us
  between operations: 14.1 us -> 0.71 us
    psum x2 -> x0, blocking collectives: 133 us -> none  [the longest x1 69.6 us: local(): first_sum, outer_sum = lax.psum((first_sum, outer_sum), ('seq', 'sub'))]
    pmax x1 -> x0, blocking collectives: 64.2 us -> none  [local(): peak = lax.pmax(local_peak, ('seq', 'sub'))]
    psum x1 -> x0, waiting for transfers between devices: 55.3 us -> none  [local(): first_sum, outer_sum = lax.psum((first_sum, outer_sum), ('seq', 'sub'))]
    dot_general x9 -> x0, matrix products: 42.3 us -> none  [the longest x8 32.5 us: block_logits(): mixed = jnp.dot(keyblk, sigma_cat[grp], preferred_element_type=jnp.float32)]
    all_to_all x0 -> x2, blocking collectives: none -> 33 us  [the longest x1 19.5 us: local(): mine = lax.all_to_all(packed, ('z', 'y'), 0, 0)]
    pallas_call x0 -> x6, Pallas kernels: none -> 30.1 us  [the longest x2 19.7 us: logits(): pl.pallas_call(functools.partial(logits_kernel, own), in_specs=[SMEM, VME...]
    convert_element_type x8 -> x0, local copies, waits for them, and re-layouts: 17.9 us -> none  [block_logits(): keyf = keyblk.astype(jnp.float32)]
    reduce_sum x4 -> x0, other arithmetic: 12.1 us -> none  [the longest x1 9.85 us: local(): vnorm = jnp.sqrt(jnp.mean(vals * vals, axis=2)).T]
  transfers between devices with their start and end apart: 1 -> 2, of which waited for: 1 -> 1; matrix products, arithmetic and copies ran while one was open for 8% -> 0% of each run, Pallas kernels for 0% -> 20%
where the time goes in v2:
time: 84.6 us; the launch traced here: 84.3 us
  blocking collectives  33 us (39%)
  Pallas kernels  30.1 us (36%)
  starting transfers between devices  13.4 us (16%)
  waiting for transfers between devices  7.08 us (8%)
    pallas_call x2, Pallas kernels, logits(): pl.pallas_call(functools.partial(logits_kernel, own), in_specs=[SMEM, VME...  19.7 us
    all_to_all x1, blocking collectives, local(): mine = lax.all_to_all(packed, ('z', 'y'), 0, 0)  19.5 us
    all_to_all x1, blocking collectives, local(): every = lax.all_to_all(st, AXES, 0, 0)  13.5 us
    all_to_all x1, starting transfers between devices, local(): rotated = lax.all_to_all(sent, AXES, 0, 0)  11.5 us
    all_to_all x1, waiting for transfers between devices, local(): rotated = lax.all_to_all(sent, AXES, 0, 0)  7.08 us
    pallas_call x1, Pallas kernels, local(): pl.pallas_call(prep_kernel, grid=(n // block,), in_specs=[pl.BlockSpec((b...  6.9 us
    ppermute x1, starting transfers between devices, local(): other = lax.ppermute(mine, 'c', [(0, 1), (1, 0)])  1.93 us
    pallas_call x1, Pallas kernels, local(): pl.pallas_call(rotate_kernel, in_specs=[HBM, HBM], out_specs=VMEM, out_sh...  1.78 us
  transfers between devices with their start and end apart: 2, of which 1 were waited for; matrix products, arithmetic and copies ran while one was open for 0% of the time, Pallas kernels for 20%

profile of v2, /device:TPU:1, one launch (start us, length us, event | category | flops | bytes accessed | tf_op | source)
XLA Modules:
  0.0 84.3 jit_solution(14507599004700836432)
XLA Ops:
  0.0 1.8 %rotate.1 = f32[128,8,128]{2,1,0:T(8,128)} custom-call(s32[4]{0:T(128)} %pos_hbm.1, bf16[4,8192]{1,0:T(4,128)(2,1)} %q_hbm.1), custom_call_target="tpu_custom_call" | custom-call | tf_op jit(solution)/shard_map/rotate/pallas_call | solution.py:213
  1.8 11.5 %all-to-all-start = ((f32[128,8,128]{2,1,0:T(8,128)}), f32[128,8,128]{2,1,0:T(8,128)S(1)}, u32[]{:S(2)}, u32[]{:S(2)}) async-start(f32[128,8,128]{2,1,0:T(8,128)} %rotate.1), calls=%async_computation | async-start | bytes 1048576 | tf_op jit(solution)/shard_map/all_to_all | solution.py:226
  13.3 6.9 %prep.1 = (bf16[256,4096]{1,0:T(8,128)(2,1)}, bf16[256,4096]{1,0:T(8,128)(2,1)}, f32[4,4096]{1,0:T(4,128)}) custom-call(bf16[4096,512]{1,0:T(8,128)(2,1)} %k_ref.1, bf16[4096,512]{1,0:T(8,128)(2,1)} %v_ref.1), custom_call_target="tpu_custom_call" | custom-call | flops 2147483648 | bytes 12582912 | tf_op jit(solution)/shard_map/prep/pallas_call | solution.py:231
  20.2 0.0 copy-start.2
  20.2 7.1 %all-to-all-done.r_ref = f32[128,8,128]{2,1,0:T(8,128)S(1)} async-done(((f32[128,8,128]{2,1,0:T(8,128)}), f32[128,8,128]{2,1,0:T(8,128)S(1)}, u32[]{:S(2)}, u32[]{:S(2)}) %all-to-all-start) | async-done | bytes 524320 | tf_op jit(solution)/shard_map/all_to_all | solution.py:226
  27.3 0.8 stats.1
  28.0 19.5 %all_to_all.21.p_ref = f32[16,136,128]{2,1,0:T(8,128)S(1)} all-to-all(f32[16,136,128]{2,1,0:T(8,128)S(1)} %stats.1), channel_id=1, replica_groups=mesh['z'=4,'y'=4,'c'=2,'x'=4] {'z','y'}, dimensions={0} | all-to-all | bytes 2228224 | tf_op jit(solution)/shard_map/all_to_all | solution.py:251
  47.5 1.9 %collective-permute-start = (f32[16,136,128]{2,1,0:T(8,128)S(1)}, f32[16,136,128]{2,1,0:T(8,128)S(1)}, u32[]{:S(2)}, u32[]{:S(2)}) collective-permute-start(f32[16,136,128]{2,1,0:T(8,128)S(1)} %all_to_all.21.p_ref), channel_id=1, source_target_pairs={{0,4},{4,0},{1,5},{5,1},{2,6},{6,2},{3,7},{7,3},{8,12},{12,8},{9,1... | collective-permute-start | bytes 3342344 | tf_op jit(solution)/shard_map/ppermute | solution.py:252
  50.1 0.0 copy-done.2
  50.1 0.0 copy-start.1
  50.1 9.8 %logits_own.1 = (f32[32,4096]{1,0:T(8,128)S(1)}, f32[8,128]{1,0:T(8,128)S(1)}) custom-call(s32[1]{0:T(128)S(6)} %copy.7.len_ref, f32[16,136,128]{2,1,0:T(8,128)S(1)} %all_to_all.21.p_ref, bf16[256,4096]{1,0:T(8,128)(2,1)S(1)} %copy-done.2), custom_call_target="tpu_custom_call" | custom-call | flops 4294967296 | bytes 4194304 | tf_op jit(solution)/shard_map/logits_own/pallas_call | solution.py:256
  59.9 0.0 collective-permute-done.p_ref
  60.0 0.0 copy-done.1
  60.0 0.0 copy-start
  60.0 9.8 %logits_other.1 = (f32[32,4096]{1,0:T(8,128)S(1)}, f32[128,128]{1,0:T(8,128)S(1)}) custom-call(s32[1]{0:T(128)S(6)} %copy.7.len_ref, f32[16,136,128]{2,1,0:T(8,128)S(1)} %collective-permute-done.p_ref, bf16[256,4096]{1,0:T(8,128)(2,1)S(1)} %copy-done.1, f32[8,128]{1,0:T(8,128)S(1)} %get-tuple-element.22.refs_0_), custom_call_target="tpu_custom_call" | custom-call | flops 4294967296 | bytes 4194304 | tf_op jit(solution)/shard_map/logits_other/pallas_call | solution.py:256
  69.8 13.5 %all_to_all.22 = f32[128,1,128]{2,1,0:T(1,128)S(1)} all-to-all(f32[128,1,128]{2,1,0:T(1,128)S(1)} %bitcast.4), channel_id=1, replica_groups=mesh['z'=4,'y'=4,'c'=2,'x'=4] {'z','y','c','x'}, dimensions={0} | all-to-all | bytes 131072 | tf_op jit(solution)/shard_map/all_to_all | solution.py:274
  83.3 0.0 copy-done
  83.3 1.0 %scores.1 = f32[4,4096]{1,0:T(4,128)} custom-call(f32[128,128]{1,0:T(8,128)S(1)} %bitcast.5, f32[128,128]{1,0:T(8,128)S(1)} %get-tuple-element.23.mine_ref, f32[32,4096]{1,0:T(8,128)S(1)} %get-tuple-element.24.wa_ref, f32[32,4096]{1,0:T(8,128)S(1)} %get-tuple-element.25.wb_ref, f32[4,4096]{1,0:T(4,128)S(1)} %copy-done), custom_call_target="tpu_custom_call" | custom-call | tf_op jit(solution)/shard_map/scores/pallas_call | solution.py:276
Async XLA Ops:
  1.8 25.5 %all-to-all-start = ((f32[128,8,128]{2,1,0:T(8,128)}), f32[128,8,128]{2,1,0:T(8,128)S(1)}, u32[]{:S(2)}, u32[]{:S(2)}) async-start(f32[128,8,128]{2,1,0:T(8,128)} %rotate.1), calls=%async_computation | async-start | bytes 1048576 | tf_op jit(solution)/shard_map/all_to_all | solution.py:226
  20.2 29.9 %copy-start.2 = (bf16[256,4096]{1,0:T(8,128)(2,1)S(1)}, bf16[256,4096]{1,0:T(8,128)(2,1)}, u32[]{:S(2)}) copy-start(bf16[256,4096]{1,0:T(8,128)(2,1)} %get-tuple-element.21.kt_ref) | copy-start | bytes 6291460
  47.5 12.4 %collective-permute-start = (f32[16,136,128]{2,1,0:T(8,128)S(1)}, f32[16,136,128]{2,1,0:T(8,128)S(1)}, u32[]{:S(2)}, u32[]{:S(2)}) collective-permute-start(f32[16,136,128]{2,1,0:T(8,128)S(1)} %all_to_all.21.p_ref), channel_id=1, source_target_pairs={{0,4},{4,0},{1,5},{5,1},{2,6},{6,2},{3,7},{7,3},{8,12},{12,8},{9,1... | collective-permute-start | bytes 3342344 | tf_op jit(solution)/shard_map/ppermute | solution.py:252
  50.1 9.8 %copy-start.1 = (bf16[256,4096]{1,0:T(8,128)(2,1)S(1)}, bf16[256,4096]{1,0:T(8,128)(2,1)}, u32[]{:S(2)}) copy-start(bf16[256,4096]{1,0:T(8,128)(2,1)} %get-tuple-element.20.kt_ref) | copy-start | bytes 6291460
  60.0 23.4 %copy-start = (f32[4,4096]{1,0:T(4,128)S(1)}, f32[4,4096]{1,0:T(4,128)}, u32[]{:S(2)}) copy-start(f32[4,4096]{1,0:T(4,128)} %get-tuple-element.26.vn_ref) | copy-start | bytes 196612

commit v3 on v2

v3 whole, which is shorter than its diff:
```python
import functools
import math

import jax
import jax.numpy as jnp
from jax import lax
from jax.experimental import pallas as pl
from jax.experimental.pallas import tpu as pltpu
from jax.sharding import Mesh
from jax.sharding import PartitionSpec as P

H = 64
KVH = 4
HD = 128
QN = 512
GROUP = H // KVH
HALF = HD // 2
AXES = ("z", "y", "c", "x")
NZ, NY, NC, NX = 4, 4, 2, 4
DEVICES = NZ * NY * NC * NX
OWNERS = NZ * NY
PLANES = OWNERS * NC
CHUNKS = H // PLANES
PACK = HALF + 8
OWN_HEADS = H // NC
PARTS = ((0, 0), (0, 1), (1, 0), (1, 1))
F32 = jnp.float32
BF16 = jnp.bfloat16
VMEM = pl.BlockSpec(memory_space=pltpu.VMEM)
SMEM = pl.BlockSpec(memory_space=pltpu.SMEM)
HBM = pl.BlockSpec(memory_space=pltpu.HBM)


def iota(shape, dim):
    return lax.broadcasted_iota(jnp.int32, shape, dim)


def rotate_kernel(pos_hbm, q_hbm, out_ref, pos_ref, q_ref, sems):
    nq = q_ref.shape[0]
    pos_copy = pltpu.make_async_copy(pos_hbm, pos_ref, sems.at[0])
    q_copy = pltpu.make_async_copy(q_hbm, q_ref, sems.at[1])
    pos_copy.start()
    q_copy.start()
    query, lane = iota((nq, HD), 0), iota((nq, HD), 1)
    position = jnp.zeros((nq, HD), F32)
    pos_copy.wait()
    for i in range(nq):
        position = jnp.where(query == i, pos_ref[i].astype(F32), position)
    freqs = jnp.exp(-lax.rem(lane, HALF).astype(F32) * (2.0 * math.log(1000000.0) / HD))
    angle = position * freqs
    cos, sin = jnp.cos(angle), jnp.sin(angle)
    sin = jnp.where(lane < HALF, -sin, sin)
    q_copy.wait()
    for chunk in range(CHUNKS):
        for plane in range(PLANES):
            zy, core = divmod(plane, NC)
            head = core * OWN_HEADS + chunk * GROUP + zy
            v = q_ref[:, head * HD : (head + 1) * HD].astype(F32)
            r = v * cos + pltpu.roll(v, HALF, 1) * sin
            for x in range(chunk, NX, CHUNKS):
                out_ref[plane * NX + x] = r


def stats_kernel(r_ref, out_ref):
    half = r_ref.shape[0] // 2
    x = jnp.concatenate([r_ref[:half], r_ref[half:]], axis=1).reshape(QN, HD)
    row_h, lane_h = iota((HALF, HD), 0), iota((HALF, HD), 1)
    eye = iota((HD, HD), 0) == iota((HD, HD), 1)
    second = lax.dot_general(
        x, x, (((0,), (0,)), ((), ())), precision=lax.Precision.HIGHEST, preferred_element_type=F32
    )
    mean = jnp.sum(x, axis=0, keepdims=True) * (1.0 / QN)
    mean_col = jnp.sum(jnp.where(eye, mean, 0.0), axis=1, keepdims=True)
    sigma = second * (1.0 / QN) - mean_col * mean
    diag = jnp.sum(jnp.where(eye, sigma, 0.0), axis=0, keepdims=True)
    packed = jnp.where(row_h < lane_h, sigma[:HALF], pltpu.roll(sigma[HALF:], HALF, 1))
    tail = jnp.concatenate([mean, diag, jnp.zeros((PACK - HALF - 2, HD), F32)], axis=0)
    for o in range(OWNERS):
        out_ref[o, :HALF, :] = packed
        out_ref[o, HALF:, :] = tail


def place(far, other):
    chunk, side = lax.rem(lax.axis_index("x"), CHUNKS), lax.axis_index("c")
    return (1 - chunk if far else chunk), (1 - side if other else side)


def prep_kernel(k_ref, v_ref, *refs):
    kt_refs, vn_ref = refs[:-1], refs[-1]
    for part, kt_ref in zip(PARTS, kt_refs):
        chunk, side = place(*part)
        low, high = k_ref[:, : CHUNKS * HD], k_ref[:, CHUNKS * HD :]
        k = jnp.where(side == 0, low, high)
        kt_ref[...] = jnp.where(chunk == 0, k[:, :HD], k[:, HD:]).T
    ones = jnp.ones((8, HD), BF16)
    nt = (((1,), (1,)), ((), ()))
    for g in range(KVH):
        v = v_ref[:, g * HD : (g + 1) * HD].astype(F32)
        sq = v * v
        hi = sq.astype(BF16)
        lo = (sq - hi.astype(F32)).astype(BF16)
        s = lax.dot_general(ones, hi, nt, preferred_element_type=F32)
        s = s + lax.dot_general(ones, lo, nt, preferred_element_type=F32)
        vn_ref[g : g + 1, :] = jnp.sqrt(s[:1] * (1.0 / HD))


def unpack(p_ref, w_ref, mu_ref):
    row, lane = iota((HALF, HD), 0), iota((HALF, HD), 1)
    down = lane - HALF
    means = []
    for h in range(GROUP):
        packed, tail = p_ref[h, :HALF, :], p_ref[h, HALF:, :]
        means.append(tail[0:1])
        diag = tail[1:2]
        top = jnp.where(row < lane, 2.0 * packed, jnp.where(row == lane, diag, 0.0))
        low = jnp.where(down < row, 2.0 * pltpu.roll(packed, HALF, 1), jnp.where(down == row, diag, 0.0))
        low = jnp.where(down >= 0, low, 0.0)
        w_ref[h * HD : h * HD + HALF, :] = top.astype(BF16)
        w_ref[h * HD + HALF : (h + 1) * HD, :] = low.astype(BF16)
    mean = jnp.concatenate(means, axis=0)
    m1 = mean.astype(BF16)
    rest = mean - m1.astype(F32)
    m2 = rest.astype(BF16)
    m3 = (rest - m2.astype(F32)).astype(BF16)
    mu_ref[0:GROUP, :] = m1
    mu_ref[GROUP : 2 * GROUP, :] = m2
    mu_ref[2 * GROUP :, :] = m3


def logits_kernel(part, len_ref, p_ref, kt_ref, *refs):
    w_out, st_out, w_ref, mu_ref = refs[-4:]
    chunk, side = place(*part)
    width = kt_ref.shape[1]
    step = 256
    unpack(p_ref, w_ref, mu_ref)
    for s in range(0, width, step):
        kt = kt_ref[:, s : s + step]
        kf = kt.astype(F32)
        lin = jnp.dot(mu_ref[...], kt, preferred_element_type=F32)
        lin = (lin[:GROUP] + lin[GROUP : 2 * GROUP]) + lin[2 * GROUP :]
        quad = []
        for h in range(GROUP):
            m = jnp.dot(w_ref[h * HD : (h + 1) * HD, :], kt, preferred_element_type=F32)
            quad.append(jnp.sum(m * kf, axis=0, keepdims=True))
        quad = jnp.concatenate(quad, axis=0)
        w_out[:, s : s + step] = quad * (0.5 / HD) + lin * (1.0 / math.sqrt(HD))
    lg = w_out[...]
    live = lax.axis_index(AXES) * width + iota(lg.shape, 1) < len_ref[0]
    peak = jnp.max(jnp.where(live, lg, -1e30), axis=1, keepdims=True)
    w = jnp.where(live, jnp.exp(jnp.where(live, lg - peak, 0.0)), 0.0)
    w_out[...] = w
    total = jnp.sum(w, axis=1, keepdims=True)
    shape = (GROUP, 2 * H)
    lane, at = iota(shape, 1), side * OWN_HEADS + chunk * GROUP + iota(shape, 0)
    both = jnp.where(lane == at, peak, 0.0) + jnp.where(lane == at + H, total, 0.0)
    st = jnp.sum(both, axis=0, keepdims=True)
    if len(refs) > 4:
        st = st + refs[0][0:1, :]
    st_out[...] = jnp.broadcast_to(st, st_out.shape)


def scores_kernel(all_ref, mine_ref, *refs):
    w_refs, vn_ref, out_ref = refs[:-2], refs[-2], refs[-1]
    every = all_ref[...]
    valid = iota(every.shape, 1) < H
    peak = jnp.max(every, axis=0, keepdims=True)
    sums = pltpu.roll(every, H, 1)
    total = jnp.where(valid, jnp.exp(jnp.where(valid, every - peak, 0.0)) * sums, 0.0)
    total = jnp.sum(total, axis=0, keepdims=True)
    ok = valid[:1]
    mine = jnp.exp(jnp.where(ok, mine_ref[0:1, :] - peak, 0.0))
    scale = jnp.where(ok, mine / jnp.where(ok, total, 1.0), 0.0)
    shape = (GROUP, 2 * H)
    width = out_ref.shape[1]

    def sums_of(w_ref, part):
        chunk, side = place(*part)
        pick = iota(shape, 1) == side * OWN_HEADS + chunk * GROUP + iota(shape, 0)
        column = jnp.sum(jnp.where(pick, scale, 0.0), axis=1, keepdims=True)
        return side * CHUNKS + chunk, jnp.sum(w_ref[...] * column, axis=0, keepdims=True)

    group = iota(out_ref.shape, 0)
    out = jnp.zeros(out_ref.shape, F32)
    for part, w_ref in zip(PARTS, w_refs):
        which, row = sums_of(w_ref, part)
        out = jnp.where(group == which, row, out)
    out_ref[...] = out * (width * DEVICES / GROUP) * vn_ref[...]


def params(mib):
    return pltpu.CompilerParams(vmem_limit_bytes=mib * 2**20)


def local(queries, query_positions, keys, cache_values, cache_length):
    n = keys.shape[0]
    nq = queries.shape[0]
    sent = pl.pallas_call(
        rotate_kernel,
        in_specs=[HBM, HBM],
        out_specs=VMEM,
        out_shape=jax.ShapeDtypeStruct((DEVICES, nq, HD), F32),
        scratch_shapes=[
            pltpu.SMEM((nq,), jnp.int32),
            pltpu.VMEM(queries.shape, BF16),
            pltpu.SemaphoreType.DMA((2,)),
        ],
        compiler_params=params(58),
        name="rotate",
    )(query_positions, queries)
    rotated = lax.all_to_all(sent, AXES, 0, 0)

    block = 1024
    turned = pl.BlockSpec((HD, block), lambda i: (0, i))
    *keys_t, vnorm = pl.pallas_call(
        prep_kernel,
        grid=(n // block,),
        in_specs=[pl.BlockSpec((block, KVH * HD), lambda i: (i, 0))] * 2,
        out_specs=[turned] * KVH + [pl.BlockSpec((KVH, block), lambda i: (0, i))],
        out_shape=[jax.ShapeDtypeStruct((HD, n), BF16)] * KVH + [jax.ShapeDtypeStruct((KVH, n), F32)],
        compiler_params=params(51),
        cost_estimate=pl.CostEstimate(flops=2 * n * 512 * 512, bytes_accessed=12 * 2**20, transcendentals=0),
        name="prep",
    )(keys, cache_values)
    rotated, keys_t, vnorm = lax.optimization_barrier((rotated, keys_t, vnorm))

    packed = pl.pallas_call(
        stats_kernel,
        in_specs=[VMEM],
        out_specs=VMEM,
        out_shape=jax.ShapeDtypeStruct((OWNERS, PACK, HD), F32),
        compiler_params=params(16),
        name="stats",
    )(rotated)
    swap = [(0, 1), (1, 0)]
    ring = [(x, (x + 1) % NX) for x in range(NX)] + [(NX + x, NX + (x - 1) % NX) for x in range(NX)]
    mine = lax.all_to_all(packed, ("z", "y"), 0, 0)
    far = lax.ppermute(mine, ("c", "x"), ring)
    stats = [mine, lax.ppermute(mine, "c", swap)]

    weights, st = [], ()
    for i, part in enumerate(PARTS):
        w, now = pl.pallas_call(
            functools.partial(logits_kernel, part),
            in_specs=[SMEM] + [VMEM] * (2 + len(st)),
            out_specs=[VMEM, VMEM],
            out_shape=[
                jax.ShapeDtypeStruct((GROUP, n), F32),
                jax.ShapeDtypeStruct((DEVICES if i == KVH - 1 else 8, 2 * H), F32),
            ],
            scratch_shapes=[pltpu.VMEM((GROUP * HD, HD), BF16), pltpu.VMEM((3 * GROUP, HD), BF16)],
            compiler_params=params(16),
            cost_estimate=pl.CostEstimate(
                flops=2 * n * GROUP * HD * HD, bytes_accessed=2 * 2**20, transcendentals=n * GROUP
            ),
            name="logits",
        )(cache_length, stats[i], keys_t[i], *st)
        weights.append(w)
        if i == NC - 1:
            far, now = lax.optimization_barrier((far, now))
            stats += [far, lax.ppermute(far, "c", swap)]
        st = (now,)
    every = lax.all_to_all(st[0], AXES, 0, 0)

    return pl.pallas_call(
        scores_kernel,
        in_specs=[VMEM] * (3 + KVH),
        out_specs=VMEM,
        out_shape=jax.ShapeDtypeStruct((KVH, n), F32),
        compiler_params=params(16),
        name="scores",
    )(every, st[0], *weights, vnorm)


def solution(mesh):
    fine = Mesh(mesh.devices.reshape(NZ, NY, NC, NX), AXES)
    return jax.shard_map(
        local,
        mesh=fine,
        in_specs=(P(AXES, None), P(AXES), P(AXES, None), P(AXES, None), P()),
        out_specs=P(None, AXES),
        check_vma=False,
    )
```

time: 84.6 us -> 78.8 us (0.931)
  blocking collectives: 33 us -> 27.8 us
  waiting for transfers between devices: 7.08 us -> 4.71 us
  starting transfers between devices: 13.4 us -> 15.6 us
    all_to_all x1, blocking collectives: 19.5 us -> 14.2 us  [local(): mine = lax.all_to_all(packed, ('z', 'y'), 0, 0)]
    all_to_all x1, waiting for transfers between devices: 7.08 us -> 4.7 us  [local(): rotated = lax.all_to_all(sent, AXES, 0, 0)]
    ppermute x1 -> x3, starting transfers between devices: 1.93 us -> 4.08 us  [the longest x1 2.02 us: local(): far = lax.ppermute(mine, ('c', 'x'), ring)]
    pallas_call x3 -> x5, Pallas kernels: 20.7 us -> 20.9 us  [the longest x4 19.9 us: local(): pl.pallas_call(functools.partial(logits_kernel, part), in_specs=[SMEM] +...]
  transfers between devices with their start and end apart: 2 -> 4, of which waited for: 1 -> 1; matrix products, arithmetic and copies ran while one was open for 0% -> 0% of each run, Pallas kernels for 20% -> 27%
where the time goes in v3:
time: 78.8 us; the launch traced here: 78.5 us
  Pallas kernels  29.7 us (38%)
  blocking collectives  27.8 us (35%)
  starting transfers between devices  15.6 us (20%)
  waiting for transfers between devices  4.71 us (6%)
    pallas_call x4, Pallas kernels, local(): pl.pallas_call(functools.partial(logits_kernel, part), in_specs=[SMEM] +...  19.9 us
    all_to_all x1, blocking collectives, local(): mine = lax.all_to_all(packed, ('z', 'y'), 0, 0)  14.2 us
    all_to_all x1, blocking collectives, local(): every = lax.all_to_all(st[0], AXES, 0, 0)  13.6 us
    all_to_all x1, starting transfers between devices, local(): rotated = lax.all_to_all(sent, AXES, 0, 0)  11.5 us
    pallas_call x1, Pallas kernels, local(): pl.pallas_call(prep_kernel, grid=(n // block,), in_specs=[pl.BlockSpec((b...  6.66 us
    all_to_all x1, waiting for transfers between devices, local(): rotated = lax.all_to_all(sent, AXES, 0, 0)  4.7 us
    ppermute x1, starting transfers between devices, local(): far = lax.ppermute(mine, ('c', 'x'), ring)  2.02 us
    ppermute x1, starting transfers between devices, local(): stats = [mine, lax.ppermute(mine, 'c', swap)]  1.75 us
  transfers between devices with their start and end apart: 4, of which 1 were waited for; matrix products, arithmetic and copies ran while one was open for 0% of the time, Pallas kernels for 27%

profile of v3, /device:TPU:1, one launch (start us, length us, event | category | flops | bytes accessed | tf_op | source)
XLA Modules:
  0.0 78.5 jit_solution(6888042576665712041)
XLA Ops:
  0.0 1.7 %rotate.1 = f32[128,4,128]{2,1,0:T(4,128)} custom-call(s32[4]{0:T(128)} %pos_hbm.1, bf16[4,8192]{1,0:T(4,128)(2,1)} %q_hbm.1), custom_call_target="tpu_custom_call" | custom-call | tf_op jit(solution)/shard_map/rotate/pallas_call | solution.py:197
  1.7 11.5 %all-to-all-start = ((f32[128,4,128]{2,1,0:T(4,128)}), f32[128,4,128]{2,1,0:T(4,128)S(1)}, u32[]{:S(2)}, u32[]{:S(2)}) async-start(f32[128,4,128]{2,1,0:T(4,128)} %rotate.1), calls=%async_computation | async-start | bytes 524288 | tf_op jit(solution)/shard_map/all_to_all | solution.py:210
  13.2 6.7 %prep.1 = (bf16[128,4096]{1,0:T(8,128)(2,1)S(1)}, bf16[128,4096]{1,0:T(8,128)(2,1)S(1)}, bf16[128,4096]{1,0:T(8,128)(2,1)}, bf16[128,4096]{1,0:T(8,128)(2,1)}, f32[4,4096]{1,0:T(4,128)S(1)}) custom-call(bf16[4096,512]{1,0:T(8,128)(2,1)} %k_ref.1, bf16[4096,512]{1,0:T(8,128)(2,1)} %v_ref.1), custom_call_target="tpu_custom_call" | custom-call | flops 2147483648 | bytes 12582912 | tf_op jit(solution)/shard_map/prep/pallas_call | solution.py:214
  19.8 4.7 %all-to-all-done.r_ref = f32[128,4,128]{2,1,0:T(4,128)S(1)} async-done(((f32[128,4,128]{2,1,0:T(4,128)}), f32[128,4,128]{2,1,0:T(4,128)S(1)}, u32[]{:S(2)}, u32[]{:S(2)}) %all-to-all-start) | async-done | bytes 262176 | tf_op jit(solution)/shard_map/all_to_all | solution.py:210
  24.5 0.5 stats.1
  25.0 14.2 %all_to_all.21.p_ref = f32[16,72,128]{2,1,0:T(8,128)S(1)} all-to-all(f32[16,72,128]{2,1,0:T(8,128)S(1)} %stats.1), channel_id=1, replica_groups=mesh['z'=4,'y'=4,'c'=2,'x'=4] {'z','y'}, dimensions={0} | all-to-all | bytes 1179648 | tf_op jit(solution)/shard_map/all_to_all | solution.py:236
  39.2 1.8 %collective-permute-start.1 = (f32[16,72,128]{2,1,0:T(8,128)S(1)}, f32[16,72,128]{2,1,0:T(8,128)S(1)}, u32[]{:S(2)}, u32[]{:S(2)}) collective-permute-start(f32[16,72,128]{2,1,0:T(8,128)S(1)} %all_to_all.21.p_ref), channel_id=1, source_target_pairs={{0,4},{4,0},{1,5},{5,1},{2,6},{6,2},{3,7},{7,3},{8,12},{12,8},{9,1... | collective-permute-start | bytes 1769480 | tf_op jit(solution)/shard_map/ppermute | solution.py:238
  41.0 2.0 %collective-permute-start = (f32[16,72,128]{2,1,0:T(8,128)S(1)}, f32[16,72,128]{2,1,0:T(8,128)S(1)}, u32[]{:S(2)}, u32[]{:S(2)}) collective-permute-start(f32[16,72,128]{2,1,0:T(8,128)S(1)} %all_to_all.21.p_ref), channel_id=1, source_target_pairs={{0,1},{1,2},{2,3},{3,0},{4,7},{5,4},{6,5},{7,6},{8,9},{9,10},{10,1... | collective-permute-start | bytes 1769480 | tf_op jit(solution)/shard_map/ppermute | solution.py:237
  43.7 5.0 %logits.4 = (f32[16,4096]{1,0:T(8,128)S(1)}, f32[8,128]{1,0:T(8,128)S(1)}) custom-call(s32[1]{0:T(128)S(6)} %copy.7.len_ref, f32[16,72,128]{2,1,0:T(8,128)S(1)} %all_to_all.21.p_ref, bf16[128,4096]{1,0:T(8,128)(2,1)S(1)} %get-tuple-element.33.kt_ref), custom_call_target="tpu_custom_call" | custom-call | flops 2147483648 | bytes 2097152 | tf_op jit(solution)/shard_map/logits/pallas_call | solution.py:242
  48.6 0.0 copy-start.1
  48.6 0.0 collective-permute-done.1.p_ref
  48.6 5.0 %logits.5 = (f32[16,4096]{1,0:T(8,128)S(1)}, f32[8,128]{1,0:T(8,128)S(1)}) custom-call(s32[1]{0:T(128)S(6)} %copy.7.len_ref, f32[16,72,128]{2,1,0:T(8,128)S(1)} %collective-permute-done.1.p_ref, bf16[128,4096]{1,0:T(8,128)(2,1)S(1)} %get-tuple-element.32.kt_ref, f32[8,128]{1,0:T(8,128)S(1)} %get-tuple-element.34.refs_0_), custom_call_target="tpu_custom_call" | custom-call | flops 2147483648 | bytes 2097152 | tf_op jit(solution)/shard_map/logits/pallas_call | solution.py:242
  53.6 0.0 copy-start
  53.6 0.0 collective-permute-done.p_ref
  53.6 0.3 collective-permute-start.2
  53.9 0.0 copy-done.1
  53.9 5.0 %logits.6 = (f32[16,4096]{1,0:T(8,128)S(1)}, f32[8,128]{1,0:T(8,128)S(1)}) custom-call(s32[1]{0:T(128)S(6)} %copy.7.len_ref, f32[16,72,128]{2,1,0:T(8,128)S(1)} %collective-permute-done.p_ref, bf16[128,4096]{1,0:T(8,128)(2,1)S(1)} %copy-done.1, f32[8,128]{1,0:T(8,128)S(1)} %get-tuple-element.39.refs_0_), custom_call_target="tpu_custom_call" | custom-call | flops 2147483648 | bytes 2097152 | tf_op jit(solution)/shard_map/logits/pallas_call | solution.py:242
  58.9 0.0 collective-permute-done.2.p_ref
  58.9 0.0 copy-done
  58.9 5.0 %logits.7 = (f32[16,4096]{1,0:T(8,128)S(1)}, f32[128,128]{1,0:T(8,128)S(1)}) custom-call(s32[1]{0:T(128)S(6)} %copy.7.len_ref, f32[16,72,128]{2,1,0:T(8,128)S(1)} %collective-permute-done.2.p_ref, bf16[128,4096]{1,0:T(8,128)(2,1)S(1)} %copy-done, f32[8,128]{1,0:T(8,128)S(1)} %get-tuple-element.40.refs_0_), custom_call_target="tpu_custom_call" | custom-call | flops 2147483648 | bytes 2097152 | tf_op jit(solution)/shard_map/logits/pallas_call | solution.py:242
  63.9 13.6 %all_to_all.22 = f32[128,1,128]{2,1,0:T(1,128)S(1)} all-to-all(f32[128,1,128]{2,1,0:T(1,128)S(1)} %bitcast.4), channel_id=1, replica_groups=mesh['z'=4,'y'=4,'c'=2,'x'=4] {'z','y','c','x'}, dimensions={0} | all-to-all | bytes 131072 | tf_op jit(solution)/shard_map/all_to_all | solution.py:262
  77.5 1.0 %scores.1 = f32[4,4096]{1,0:T(4,128)} custom-call(f32[128,128]{1,0:T(8,128)S(1)} %bitcast.5, f32[128,128]{1,0:T(8,128)S(1)} %get-tuple-element.41.mine_ref, f32[16,4096]{1,0:T(8,128)S(1)} %get-tuple-element.42.refs_0_, f32[16,4096]{1,0:T(8,128)S(1)} %get-tuple-element.43.refs_1_, f32[16,4096]{1,0:T(8,128)S(1)} %get-tuple-element.44.refs_2_, ...), custom_call_target="tpu_custom_call" | custom-call | tf_op jit(solution)/shard_map/scores/pallas_call | solution.py:264
Async XLA Ops:
  1.7 22.9 %all-to-all-start = ((f32[128,4,128]{2,1,0:T(4,128)}), f32[128,4,128]{2,1,0:T(4,128)S(1)}, u32[]{:S(2)}, u32[]{:S(2)}) async-start(f32[128,4,128]{2,1,0:T(4,128)} %rotate.1), calls=%async_computation | async-start | bytes 524288 | tf_op jit(solution)/shard_map/all_to_all | solution.py:210
  39.2 9.4 %collective-permute-start.1 = (f32[16,72,128]{2,1,0:T(8,128)S(1)}, f32[16,72,128]{2,1,0:T(8,128)S(1)}, u32[]{:S(2)}, u32[]{:S(2)}) collective-permute-start(f32[16,72,128]{2,1,0:T(8,128)S(1)} %all_to_all.21.p_ref), channel_id=1, source_target_pairs={{0,4},{4,0},{1,5},{5,1},{2,6},{6,2},{3,7},{7,3},{8,12},{12,8},{9,1... | collective-permute-start | bytes 1769480 | tf_op jit(solution)/shard_map/ppermute | solution.py:238
  41.0 12.6 %collective-permute-start = (f32[16,72,128]{2,1,0:T(8,128)S(1)}, f32[16,72,128]{2,1,0:T(8,128)S(1)}, u32[]{:S(2)}, u32[]{:S(2)}) collective-permute-start(f32[16,72,128]{2,1,0:T(8,128)S(1)} %all_to_all.21.p_ref), channel_id=1, source_target_pairs={{0,1},{1,2},{2,3},{3,0},{4,7},{5,4},{6,5},{7,6},{8,9},{9,10},{10,1... | collective-permute-start | bytes 1769480 | tf_op jit(solution)/shard_map/ppermute | solution.py:237
  48.6 5.3 %copy-start.1 = (bf16[128,4096]{1,0:T(8,128)(2,1)S(1)}, bf16[128,4096]{1,0:T(8,128)(2,1)}, u32[]{:S(2)}) copy-start(bf16[128,4096]{1,0:T(8,128)(2,1)} %get-tuple-element.38.kt_ref) | copy-start | bytes 3145732
  53.6 5.3 %copy-start = (bf16[128,4096]{1,0:T(8,128)(2,1)S(1)}, bf16[128,4096]{1,0:T(8,128)(2,1)}, u32[]{:S(2)}) copy-start(bf16[128,4096]{1,0:T(8,128)(2,1)} %get-tuple-element.37.kt_ref) | copy-start | bytes 3145732
  53.6 5.3 %collective-permute-start.2 = (f32[16,72,128]{2,1,0:T(8,128)S(1)}, f32[16,72,128]{2,1,0:T(8,128)S(1)}, u32[]{:S(2)}, u32[]{:S(2)}) collective-permute-start(f32[16,72,128]{2,1,0:T(8,128)S(1)} %collective-permute-done.p_ref), channel_id=1, source_target_pairs={{0,4},{4,0},{1,5},{5,1},{2,6},{6,2},{3,7},{7,3},{8,12},{12,8},{9,1... | collective-permute-start | bytes 1769480 | tf_op jit(solution)/shard_map/ppermute | solution.py:260

commit v4 on v3

--- a/solution.py
+++ b/solution.py
@@ -23,6 +23,8 @@
 CHUNKS = H // PLANES
 PACK = HALF + 8
 OWN_HEADS = H // NC
+LAST = 8
+ROWS = HD - LAST
 PARTS = ((0, 0), (0, 1), (1, 0), (1, 1))
 F32 = jnp.float32
 BF16 = jnp.bfloat16
@@ -74,7 +76,15 @@
     sigma = second * (1.0 / QN) - mean_col * mean
     diag = jnp.sum(jnp.where(eye, sigma, 0.0), axis=0, keepdims=True)
     packed = jnp.where(row_h < lane_h, sigma[:HALF], pltpu.roll(sigma[HALF:], HALF, 1))
-    tail = jnp.concatenate([mean, diag, jnp.zeros((PACK - HALF - 2, HD), F32)], axis=0)
+    row_l, lane_l = iota((LAST, HD), 0), iota((LAST, HD), 1)
+    corner = jnp.zeros((LAST, HD), F32)
+    for i in range(LAST):
+        moved = pltpu.roll(sigma[HALF : HALF + LAST], (LAST * i - HALF) % HD, 1)
+        j = lane_l - LAST * i
+        moved = jnp.where(j < i, 2.0 * moved, moved)
+        corner = jnp.where((row_l == i) & (j >= 0) & (j <= i), moved, corner)
+    corner = jnp.sum(corner, axis=0, keepdims=True)
+    tail = jnp.concatenate([mean, diag, corner, jnp.zeros((PACK - HALF - 3, HD), F32)], axis=0)
     for o in range(OWNERS):
         out_ref[o, :HALF, :] = packed
         out_ref[o, HALF:, :] = tail
@@ -85,8 +95,10 @@
     return (1 - chunk if far else chunk), (1 - side if other else side)
 
 
-def prep_kernel(k_ref, v_ref, *refs):
-    kt_refs, vn_ref = refs[:-1], refs[-1]
+def prep_kernel(len_ref, k_ref, v_ref, *refs):
+    kt_refs, vn_ref, live_ref = refs[:-2], refs[-2], refs[-1]
+    here = pl.num_programs(0) * k_ref.shape[0]
+    live_ref[...] = jnp.full(live_ref.shape, len_ref[0] - lax.axis_index(AXES) * here, jnp.int32)
     for part, kt_ref in zip(PARTS, kt_refs):
         chunk, side = place(*part)
         low, high = k_ref[:, : CHUNKS * HD], k_ref[:, CHUNKS * HD :]
@@ -104,19 +116,22 @@
         vn_ref[g : g + 1, :] = jnp.sqrt(s[:1] * (1.0 / HD))
 
 
-def unpack(p_ref, w_ref, mu_ref):
+def unpack(p_ref, w_ref, mu_ref, corner_ref):
     row, lane = iota((HALF, HD), 0), iota((HALF, HD), 1)
     down = lane - HALF
-    means = []
+    means, corners, forms = [], [], []
     for h in range(GROUP):
         packed, tail = p_ref[h, :HALF, :], p_ref[h, HALF:, :]
         means.append(tail[0:1])
         diag = tail[1:2]
+        corners.append(tail[2:3])
         top = jnp.where(row < lane, 2.0 * packed, jnp.where(row == lane, diag, 0.0))
         low = jnp.where(down < row, 2.0 * pltpu.roll(packed, HALF, 1), jnp.where(down == row, diag, 0.0))
         low = jnp.where(down >= 0, low, 0.0)
-        w_ref[h * HD : h * HD + HALF, :] = top.astype(BF16)
-        w_ref[h * HD + HALF : (h + 1) * HD, :] = low.astype(BF16)
+        forms += [top, low[LAST:]]
+        if h % 2 == 1:
+            w_ref[(h - 1) * ROWS : (h + 1) * ROWS, :] = jnp.concatenate(forms, axis=0).astype(BF16)
+            forms = []
     mean = jnp.concatenate(means, axis=0)
     m1 = mean.astype(BF16)
     rest = mean - m1.astype(F32)
@@ -125,27 +140,45 @@
     mu_ref[0:GROUP, :] = m1
     mu_ref[GROUP : 2 * GROUP, :] = m2
     mu_ref[2 * GROUP :, :] = m3
-
-
-def logits_kernel(part, len_ref, p_ref, kt_ref, *refs):
-    w_out, st_out, w_ref, mu_ref = refs[-4:]
+    corner = jnp.concatenate(corners, axis=0).astype(BF16).astype(F32)
+    for i in range(LAST):
+        for j in range(i + 1):
+            at = LAST * i + j
+            corner_ref[at] = jnp.broadcast_to(corner[:, at : at + 1], (GROUP, HD))
+
+
+def corner_sum(corner_ref, kf):
+    width = kf.shape[1]
+    last = [jnp.broadcast_to(kf[HALF + i : HALF + i + 1], (GROUP, width)) for i in range(LAST)]
+    total = jnp.zeros((GROUP, width), F32)
+    for i in range(LAST):
+        inner = jnp.zeros((GROUP, width), F32)
+        for j in range(i + 1):
+            inner = inner + jnp.concatenate([corner_ref[LAST * i + j]] * (width // HD), axis=1) * last[j]
+        total = total + inner * last[i]
+    return total
+
+
+def logits_kernel(part, live_ref, p_ref, kt_ref, *refs):
+    w_out, st_out, w_ref, mu_ref, corner_ref = refs[-5:]
     chunk, side = place(*part)
     width = kt_ref.shape[1]
     step = 256
-    unpack(p_ref, w_ref, mu_ref)
+    unpack(p_ref, w_ref, mu_ref, corner_ref)
     for s in range(0, width, step):
         kt = kt_ref[:, s : s + step]
         kf = kt.astype(F32)
         lin = jnp.dot(mu_ref[...], kt, preferred_element_type=F32)
         lin = (lin[:GROUP] + lin[GROUP : 2 * GROUP]) + lin[2 * GROUP :]
-        quad = []
-        for h in range(GROUP):
-            m = jnp.dot(w_ref[h * HD : (h + 1) * HD, :], kt, preferred_element_type=F32)
-            quad.append(jnp.sum(m * kf, axis=0, keepdims=True))
-        quad = jnp.concatenate(quad, axis=0)
+        kr = jnp.concatenate([kf[:HALF], kf[HALF + LAST :]], axis=0)
+        m = jnp.dot(w_ref[...], kt, preferred_element_type=F32)
+        quad = [
+            jnp.sum(m[h * ROWS : (h + 1) * ROWS] * kr, axis=0, keepdims=True) for h in range(GROUP)
+        ]
+        quad = jnp.concatenate(quad, axis=0) + corner_sum(corner_ref, kf)
         w_out[:, s : s + step] = quad * (0.5 / HD) + lin * (1.0 / math.sqrt(HD))
     lg = w_out[...]
-    live = lax.axis_index(AXES) * width + iota(lg.shape, 1) < len_ref[0]
+    live = iota(lg.shape, 1) < jnp.broadcast_to(live_ref[0:1, 0:1], lg.shape)
     peak = jnp.max(jnp.where(live, lg, -1e30), axis=1, keepdims=True)
     w = jnp.where(live, jnp.exp(jnp.where(live, lg - peak, 0.0)), 0.0)
     w_out[...] = w
@@ -154,7 +187,7 @@
     lane, at = iota(shape, 1), side * OWN_HEADS + chunk * GROUP + iota(shape, 0)
     both = jnp.where(lane == at, peak, 0.0) + jnp.where(lane == at + H, total, 0.0)
     st = jnp.sum(both, axis=0, keepdims=True)
-    if len(refs) > 4:
+    if len(refs) > 5:
         st = st + refs[0][0:1, :]
     st_out[...] = jnp.broadcast_to(st, st_out.shape)
 
@@ -211,17 +244,19 @@
 
     block = 1024
     turned = pl.BlockSpec((HD, block), lambda i: (0, i))
-    *keys_t, vnorm = pl.pallas_call(
+    *keys_t, vnorm, live = pl.pallas_call(
         prep_kernel,
         grid=(n // block,),
-        in_specs=[pl.BlockSpec((block, KVH * HD), lambda i: (i, 0))] * 2,
-        out_specs=[turned] * KVH + [pl.BlockSpec((KVH, block), lambda i: (0, i))],
-        out_shape=[jax.ShapeDtypeStruct((HD, n), BF16)] * KVH + [jax.ShapeDtypeStruct((KVH, n), F32)],
+        in_specs=[SMEM] + [pl.BlockSpec((block, KVH * HD), lambda i: (i, 0))] * 2,
+        out_specs=[turned] * KVH
+        + [pl.BlockSpec((KVH, block), lambda i: (0, i)), pl.BlockSpec((8, HD), lambda i: (0, 0))],
+        out_shape=[jax.ShapeDtypeStruct((HD, n), BF16)] * KVH
+        + [jax.ShapeDtypeStruct((KVH, n), F32), jax.ShapeDtypeStruct((8, HD), jnp.int32)],
         compiler_params=params(51),
         cost_estimate=pl.CostEstimate(flops=2 * n * 512 * 512, bytes_accessed=12 * 2**20, transcendentals=0),
         name="prep",
-    )(keys, cache_values)
-    rotated, keys_t, vnorm = lax.optimization_barrier((rotated, keys_t, vnorm))
+    )(cache_length, keys, cache_values)
+    rotated, keys_t, vnorm, live = lax.optimization_barrier((rotated, keys_t, vnorm, live))
 
     packed = pl.pallas_call(
         stats_kernel,
@@ -241,19 +276,23 @@
     for i, part in enumerate(PARTS):
         w, now = pl.pallas_call(
             functools.partial(logits_kernel, part),
-            in_specs=[SMEM] + [VMEM] * (2 + len(st)),
+            in_specs=[VMEM] * (3 + len(st)),
             out_specs=[VMEM, VMEM],
             out_shape=[
                 jax.ShapeDtypeStruct((GROUP, n), F32),
                 jax.ShapeDtypeStruct((DEVICES if i == KVH - 1 else 8, 2 * H), F32),
             ],
-            scratch_shapes=[pltpu.VMEM((GROUP * HD, HD), BF16), pltpu.VMEM((3 * GROUP, HD), BF16)],
+            scratch_shapes=[
+                pltpu.VMEM((GROUP * ROWS, HD), BF16),
+                pltpu.VMEM((3 * GROUP, HD), BF16),
+                pltpu.VMEM((LAST * LAST, GROUP, HD), F32),
+            ],
             compiler_params=params(16),
             cost_estimate=pl.CostEstimate(
                 flops=2 * n * GROUP * HD * HD, bytes_accessed=2 * 2**20, transcendentals=n * GROUP
             ),
             name="logits",
-        )(cache_length, stats[i], keys_t[i], *st)
+        )(live, stats[i], keys_t[i], *st)
         weights.append(w)
         if i == NC - 1:
             far, now = lax.optimization_barrier((far, now))

time: 78.8 us -> 78.2 us (level)
  no operation moved by 1% of the time
where the time goes in v4:
time: 78.2 us; the launch traced here: 77.9 us
  Pallas kernels  29.1 us (37%)
  blocking collectives  28 us (36%)
  starting transfers between devices  16 us (20%)
  waiting for transfers between devices  4.06 us (5%)
    pallas_call x4, Pallas kernels, local(): pl.pallas_call(functools.partial(logits_kernel, part), in_specs=[VMEM] *...  19.2 us
    all_to_all x1, blocking collectives, local(): mine = lax.all_to_all(packed, ('z', 'y'), 0, 0)  14.4 us
    all_to_all x1, blocking collectives, local(): every = lax.all_to_all(st[0], AXES, 0, 0)  13.6 us
    all_to_all x1, starting transfers between devices, local(): rotated = lax.all_to_all(sent, AXES, 0, 0)  11.5 us
    pallas_call x1, Pallas kernels, local(): pl.pallas_call(prep_kernel, grid=(n // block,), in_specs=[SMEM] + [pl.Blo...  6.66 us
    all_to_all x1, waiting for transfers between devices, local(): rotated = lax.all_to_all(sent, AXES, 0, 0)  4.05 us
    ppermute x1, starting transfers between devices, local(): far = lax.ppermute(mine, ('c', 'x'), ring)  2.44 us
    ppermute x1, starting transfers between devices, local(): stats = [mine, lax.ppermute(mine, 'c', swap)]  1.79 us
  transfers between devices with their start and end apart: 4, of which 1 were waited for; matrix products, arithmetic and copies ran while one was open for 0% of the time, Pallas kernels for 27%

profile of v4, /device:TPU:1, one launch (start us, length us, event | category | flops | bytes accessed | tf_op | source)
XLA Modules:
  0.0 77.9 jit_solution(14707696161870497940)
XLA Ops:
  0.0 1.7 %rotate.1 = f32[128,4,128]{2,1,0:T(4,128)} custom-call(s32[4]{0:T(128)} %pos_hbm.1, bf16[4,8192]{1,0:T(4,128)(2,1)} %q_hbm.1), custom_call_target="tpu_custom_call" | custom-call | tf_op jit(solution)/shard_map/rotate/pallas_call | solution.py:230
  1.7 11.5 %all-to-all-start = ((f32[128,4,128]{2,1,0:T(4,128)}), f32[128,4,128]{2,1,0:T(4,128)S(1)}, u32[]{:S(2)}, u32[]{:S(2)}) async-start(f32[128,4,128]{2,1,0:T(4,128)} %rotate.1), calls=%async_computation | async-start | bytes 524288 | tf_op jit(solution)/shard_map/all_to_all | solution.py:243
  13.8 6.7 %prep.1 = (bf16[128,4096]{1,0:T(8,128)(2,1)S(1)}, bf16[128,4096]{1,0:T(8,128)(2,1)S(1)}, bf16[128,4096]{1,0:T(8,128)(2,1)}, bf16[128,4096]{1,0:T(8,128)(2,1)}, f...) custom-call(s32[1]{0:T(128)S(6)} %copy.7.len_ref, bf16[4096,512]{1,0:T(8,128)(2,1)} %k_ref.1, bf16[4096,512]{1,0:T(8,128)(2,1)} %v_ref.1), custom_call_target="tpu_custom_call" | custom-call | flops 2147483648 | bytes 12582912 | tf_op jit(solution)/shard_map/prep/pallas_call | solution.py:247
  20.5 4.1 %all-to-all-done.r_ref = f32[128,4,128]{2,1,0:T(4,128)S(1)} async-done(((f32[128,4,128]{2,1,0:T(4,128)}), f32[128,4,128]{2,1,0:T(4,128)S(1)}, u32[]{:S(2)}, u32[]{:S(2)}) %all-to-all-start) | async-done | bytes 262176 | tf_op jit(solution)/shard_map/all_to_all | solution.py:243
  24.5 0.5 stats.1
  25.1 14.4 %all_to_all.21.p_ref = f32[16,72,128]{2,1,0:T(8,128)S(1)} all-to-all(f32[16,72,128]{2,1,0:T(8,128)S(1)} %stats.1), channel_id=1, replica_groups=mesh['z'=4,'y'=4,'c'=2,'x'=4] {'z','y'}, dimensions={0} | all-to-all | bytes 1179648 | tf_op jit(solution)/shard_map/all_to_all | solution.py:271
  39.4 1.8 %collective-permute-start.1 = (f32[16,72,128]{2,1,0:T(8,128)S(1)}, f32[16,72,128]{2,1,0:T(8,128)S(1)}, u32[]{:S(2)}, u32[]{:S(2)}) collective-permute-start(f32[16,72,128]{2,1,0:T(8,128)S(1)} %all_to_all.21.p_ref), channel_id=1, source_target_pairs={{0,4},{4,0},{1,5},{5,1},{2,6},{6,2},{3,7},{7,3},{8,12},{12,8},{9,1... | collective-permute-start | bytes 1769480 | tf_op jit(solution)/shard_map/ppermute | solution.py:273
  41.2 2.4 %collective-permute-start = (f32[16,72,128]{2,1,0:T(8,128)S(1)}, f32[16,72,128]{2,1,0:T(8,128)S(1)}, u32[]{:S(2)}, u32[]{:S(2)}) collective-permute-start(f32[16,72,128]{2,1,0:T(8,128)S(1)} %all_to_all.21.p_ref), channel_id=1, source_target_pairs={{0,1},{1,2},{2,3},{3,0},{4,7},{5,4},{6,5},{7,6},{8,9},{9,10},{10,1... | collective-permute-start | bytes 1769480 | tf_op jit(solution)/shard_map/ppermute | solution.py:272
  43.7 4.8 %logits.4 = (f32[16,4096]{1,0:T(8,128)S(1)}, f32[8,128]{1,0:T(8,128)S(1)}) custom-call(s32[8,128]{1,0:T(8,128)S(1)} %get-tuple-element.34.live_ref, f32[16,72,128]{2,1,0:T(8,128)S(1)} %all_to_all.21.p_ref, bf16[128,4096]{1,0:T(8,128)(2,1)S(1)} %get-tuple-element.37.kt_ref), custom_call_target="tpu_custom_call" | custom-call | flops 2147483648 | bytes 2097152 | tf_op jit(solution)/shard_map/logits/pallas_call | solution.py:277
  48.5 0.0 copy-start.1
  48.5 0.0 collective-permute-done.1.p_ref
  48.5 4.8 %logits.5 = (f32[16,4096]{1,0:T(8,128)S(1)}, f32[8,128]{1,0:T(8,128)S(1)}) custom-call(s32[8,128]{1,0:T(8,128)S(1)} %get-tuple-element.34.live_ref, f32[16,72,128]{2,1,0:T(8,128)S(1)} %collective-permute-done.1.p_ref, bf16[128,4096]{1,0:T(8,128)(2,1)S(1)} %get-tuple-element.36.kt_ref, f32[8,128]{1,0:T(8,128)S(1)} %get-tuple-element.38.refs_0_), custom_call_target="tpu_custom_call" | custom-call | flops 2147483648 | bytes 2097152 | tf_op jit(solution)/shard_map/logits/pallas_call | solution.py:277
  53.3 0.0 copy-start
  53.3 0.0 collective-permute-done.p_ref
  53.3 0.3 collective-permute-start.2
  53.6 0.0 copy-done.1
  53.6 4.8 %logits.6 = (f32[16,4096]{1,0:T(8,128)S(1)}, f32[8,128]{1,0:T(8,128)S(1)}) custom-call(s32[8,128]{1,0:T(8,128)S(1)} %get-tuple-element.34.live_ref, f32[16,72,128]{2,1,0:T(8,128)S(1)} %collective-permute-done.p_ref, bf16[128,4096]{1,0:T(8,128)(2,1)S(1)} %copy-done.1, f32[8,128]{1,0:T(8,128)S(1)} %get-tuple-element.43.refs_0_), custom_call_target="tpu_custom_call" | custom-call | flops 2147483648 | bytes 2097152 | tf_op jit(solution)/shard_map/logits/pallas_call | solution.py:277
  58.4 0.0 collective-permute-done.2.p_ref
  58.5 0.0 copy-done
  58.5 4.8 %logits.7 = (f32[16,4096]{1,0:T(8,128)S(1)}, f32[128,128]{1,0:T(8,128)S(1)}) custom-call(s32[8,128]{1,0:T(8,128)S(1)} %get-tuple-element.34.live_ref, f32[16,72,128]{2,1,0:T(8,128)S(1)} %collective-permute-done.2.p_ref, bf16[128,4096]{1,0:T(8,128)(2,1)S(1)} %copy-done, f32[8,128]{1,0:T(8,128)S(1)} %get-tuple-element.44.refs_0_), custom_call_target="tpu_custom_call" | custom-call | flops 2147483648 | bytes 2097152 | tf_op jit(solution)/shard_map/logits/pallas_call | solution.py:277
  63.3 13.6 %all_to_all.22 = f32[128,1,128]{2,1,0:T(1,128)S(1)} all-to-all(f32[128,1,128]{2,1,0:T(1,128)S(1)} %bitcast.4), channel_id=1, replica_groups=mesh['z'=4,'y'=4,'c'=2,'x'=4] {'z','y','c','x'}, dimensions={0} | all-to-all | bytes 131072 | tf_op jit(solution)/shard_map/all_to_all | solution.py:301
  76.9 1.0 %scores.1 = f32[4,4096]{1,0:T(4,128)} custom-call(f32[128,128]{1,0:T(8,128)S(1)} %bitcast.5, f32[128,128]{1,0:T(8,128)S(1)} %get-tuple-element.45.mine_ref, f32[16,4096]{1,0:T(8,128)S(1)} %get-tuple-element.46.refs_0_, f32[16,4096]{1,0:T(8,128)S(1)} %get-tuple-element.47.refs_1_, f32[16,4096]{1,0:T(8,128)S(1)} %get-tuple-element.48.refs_2_, ...), custom_call_target="tpu_custom_call" | custom-call | tf_op jit(solution)/shard_map/scores/pallas_call | solution.py:303
Async XLA Ops:
  1.7 22.9 %all-to-all-start = ((f32[128,4,128]{2,1,0:T(4,128)}), f32[128,4,128]{2,1,0:T(4,128)S(1)}, u32[]{:S(2)}, u32[]{:S(2)}) async-start(f32[128,4,128]{2,1,0:T(4,128)} %rotate.1), calls=%async_computation | async-start | bytes 524288 | tf_op jit(solution)/shard_map/all_to_all | solution.py:243
  39.4 9.0 %collective-permute-start.1 = (f32[16,72,128]{2,1,0:T(8,128)S(1)}, f32[16,72,128]{2,1,0:T(8,128)S(1)}, u32[]{:S(2)}, u32[]{:S(2)}) collective-permute-start(f32[16,72,128]{2,1,0:T(8,128)S(1)} %all_to_all.21.p_ref), channel_id=1, source_target_pairs={{0,4},{4,0},{1,5},{5,1},{2,6},{6,2},{3,7},{7,3},{8,12},{12,8},{9,1... | collective-permute-start | bytes 1769480 | tf_op jit(solution)/shard_map/ppermute | solution.py:273
  41.2 12.1 %collective-permute-start = (f32[16,72,128]{2,1,0:T(8,128)S(1)}, f32[16,72,128]{2,1,0:T(8,128)S(1)}, u32[]{:S(2)}, u32[]{:S(2)}) collective-permute-start(f32[16,72,128]{2,1,0:T(8,128)S(1)} %all_to_all.21.p_ref), channel_id=1, source_target_pairs={{0,1},{1,2},{2,3},{3,0},{4,7},{5,4},{6,5},{7,6},{8,9},{9,10},{10,1... | collective-permute-start | bytes 1769480 | tf_op jit(solution)/shard_map/ppermute | solution.py:272
  48.5 5.1 %copy-start.1 = (bf16[128,4096]{1,0:T(8,128)(2,1)S(1)}, bf16[128,4096]{1,0:T(8,128)(2,1)}, u32[]{:S(2)}) copy-start(bf16[128,4096]{1,0:T(8,128)(2,1)} %get-tuple-element.42.kt_ref) | copy-start | bytes 3145732
  53.3 5.1 %copy-start = (bf16[128,4096]{1,0:T(8,128)(2,1)S(1)}, bf16[128,4096]{1,0:T(8,128)(2,1)}, u32[]{:S(2)}) copy-start(bf16[128,4096]{1,0:T(8,128)(2,1)} %get-tuple-element.41.kt_ref) | copy-start | bytes 3145732
  53.3 5.1 %collective-permute-start.2 = (f32[16,72,128]{2,1,0:T(8,128)S(1)}, f32[16,72,128]{2,1,0:T(8,128)S(1)}, u32[]{:S(2)}, u32[]{:S(2)}) collective-permute-start(f32[16,72,128]{2,1,0:T(8,128)S(1)} %collective-permute-done.p_ref), channel_id=1, source_target_pairs={{0,4},{4,0},{1,5},{5,1},{2,6},{6,2},{3,7},{7,3},{8,12},{12,8},{9,1... | collective-permute-start | bytes 1769480 | tf_op jit(solution)/shard_map/ppermute | solution.py:299

commit v5 on v4

--- a/solution.py
+++ b/solution.py
@@ -95,8 +95,8 @@
     return (1 - chunk if far else chunk), (1 - side if other else side)
 
 
-def prep_kernel(len_ref, k_ref, v_ref, *refs):
-    kt_refs, vn_ref, live_ref = refs[:-2], refs[-2], refs[-1]
+def turn_kernel(len_ref, k_ref, *refs):
+    kt_refs, live_ref = refs[:-1], refs[-1]
     here = pl.num_programs(0) * k_ref.shape[0]
     live_ref[...] = jnp.full(live_ref.shape, len_ref[0] - lax.axis_index(AXES) * here, jnp.int32)
     for part, kt_ref in zip(PARTS, kt_refs):
@@ -104,6 +104,9 @@
         low, high = k_ref[:, : CHUNKS * HD], k_ref[:, CHUNKS * HD :]
         k = jnp.where(side == 0, low, high)
         kt_ref[...] = jnp.where(chunk == 0, k[:, :HD], k[:, HD:]).T
+
+
+def norms_kernel(v_ref, vn_ref):
     ones = jnp.ones((8, HD), BF16)
     nt = (((1,), (1,)), ((), ()))
     for g in range(KVH):
@@ -160,7 +163,9 @@
 
 
 def logits_kernel(part, live_ref, p_ref, kt_ref, *refs):
-    w_out, st_out, w_ref, mu_ref, corner_ref = refs[-5:]
+    w_ref, mu_ref, corner_ref = refs[-3:]
+    refs = refs[:-3]
+    prev_ref, (w_out, *st_outs) = (None, refs) if part == PARTS[0] else (refs[0], refs[1:])
     chunk, side = place(*part)
     width = kt_ref.shape[1]
     step = 256
@@ -187,9 +192,10 @@
     lane, at = iota(shape, 1), side * OWN_HEADS + chunk * GROUP + iota(shape, 0)
     both = jnp.where(lane == at, peak, 0.0) + jnp.where(lane == at + H, total, 0.0)
     st = jnp.sum(both, axis=0, keepdims=True)
-    if len(refs) > 5:
-        st = st + refs[0][0:1, :]
-    st_out[...] = jnp.broadcast_to(st, st_out.shape)
+    if prev_ref is not None:
+        st = st + prev_ref[0:1, :]
+    for st_out in st_outs:
+        st_out[...] = jnp.broadcast_to(st, st_out.shape)
 
 
 def scores_kernel(all_ref, mine_ref, *refs):
@@ -243,20 +249,18 @@
     rotated = lax.all_to_all(sent, AXES, 0, 0)
 
     block = 1024
-    turned = pl.BlockSpec((HD, block), lambda i: (0, i))
-    *keys_t, vnorm, live = pl.pallas_call(
-        prep_kernel,
+    rows = pl.BlockSpec((block, KVH * HD), lambda i: (i, 0))
+    *keys_t, live = pl.pallas_call(
+        turn_kernel,
         grid=(n // block,),
-        in_specs=[SMEM] + [pl.BlockSpec((block, KVH * HD), lambda i: (i, 0))] * 2,
-        out_specs=[turned] * KVH
-        + [pl.BlockSpec((KVH, block), lambda i: (0, i)), pl.BlockSpec((8, HD), lambda i: (0, 0))],
-        out_shape=[jax.ShapeDtypeStruct((HD, n), BF16)] * KVH
-        + [jax.ShapeDtypeStruct((KVH, n), F32), jax.ShapeDtypeStruct((8, HD), jnp.int32)],
+        in_specs=[SMEM, rows],
+        out_specs=[pl.BlockSpec((HD, block), lambda i: (0, i))] * KVH + [pl.BlockSpec((8, HD), lambda i: (0, 0))],
+        out_shape=[jax.ShapeDtypeStruct((HD, n), BF16)] * KVH + [jax.ShapeDtypeStruct((8, HD), jnp.int32)],
         compiler_params=params(51),
-        cost_estimate=pl.CostEstimate(flops=2 * n * 512 * 512, bytes_accessed=12 * 2**20, transcendentals=0),
-        name="prep",
-    )(cache_length, keys, cache_values)
-    rotated, keys_t, vnorm, live = lax.optimization_barrier((rotated, keys_t, vnorm, live))
+        cost_estimate=pl.CostEstimate(flops=2 * n * 512 * 512, bytes_accessed=8 * 2**20, transcendentals=0),
+        name="turn",
+    )(cache_length, keys)
+    rotated, keys_t, live = lax.optimization_barrier((rotated, keys_t, live))
 
     packed = pl.pallas_call(
         stats_kernel,
@@ -274,14 +278,13 @@
 
     weights, st = [], ()
     for i, part in enumerate(PARTS):
-        w, now = pl.pallas_call(
+        copies = (8, DEVICES) if i == KVH - 1 else (8,)
+        w, now, *wide = pl.pallas_call(
             functools.partial(logits_kernel, part),
             in_specs=[VMEM] * (3 + len(st)),
-            out_specs=[VMEM, VMEM],
-            out_shape=[
-                jax.ShapeDtypeStruct((GROUP, n), F32),
-                jax.ShapeDtypeStruct((DEVICES if i == KVH - 1 else 8, 2 * H), F32),
-            ],
+            out_specs=[VMEM] * (1 + len(copies)),
+            out_shape=[jax.ShapeDtypeStruct((GROUP, n), F32)]
+            + [jax.ShapeDtypeStruct((rows_out, 2 * H), F32) for rows_out in copies],
             scratch_shapes=[
                 pltpu.VMEM((GROUP * ROWS, HD), BF16),
                 pltpu.VMEM((3 * GROUP, HD), BF16),
@@ -298,7 +301,18 @@
             far, now = lax.optimization_barrier((far, now))
             stats += [far, lax.ppermute(far, "c", swap)]
         st = (now,)
-    every = lax.all_to_all(st[0], AXES, 0, 0)
+    every = lax.all_to_all(wide[0], AXES, 0, 0)
+    vnorm = pl.pallas_call(
+        norms_kernel,
+        grid=(n // block,),
+        in_specs=[rows],
+        out_specs=pl.BlockSpec((KVH, block), lambda i: (0, i)),
+        out_shape=jax.ShapeDtypeStruct((KVH, n), F32),
+        compiler_params=params(51),
+        cost_estimate=pl.CostEstimate(flops=2 * n * 512 * 512, bytes_accessed=4 * 2**20, transcendentals=0),
+        name="norms",
+    )(cache_values)
+    every, vnorm = lax.optimization_barrier((every, vnorm))
 
     return pl.pallas_call(
         scores_kernel,

time: 78.2 us -> 77.8 us (level)
  blocking collectives: 28 us -> 14.2 us
  waiting for transfers between devices: 4.06 us -> 10.8 us
  Pallas kernels: 29.1 us -> 32.5 us
  starting transfers between devices: 16 us -> 19.2 us
    all_to_all x1 -> x0, blocking collectives: 13.6 us -> none  [local(): every = lax.all_to_all(st[0], AXES, 0, 0)]
    all_to_all x0 -> x1, waiting for transfers between devices: none -> 4.94 us  [local(): every = lax.all_to_all(wide[0], AXES, 0, 0)]
    all_to_all x0 -> x1, starting transfers between devices: none -> 4.43 us  [local(): every = lax.all_to_all(wide[0], AXES, 0, 0)]
    pallas_call x1 -> x2, Pallas kernels: 6.66 us -> 9.55 us  [the longest x1 4.89 us: local(): pl.pallas_call(turn_kernel, grid=(n // block,), in_specs=[SMEM, rows], ou...]
    all_to_all x1, waiting for transfers between devices: 4.05 us -> 5.82 us  [local(): rotated = lax.all_to_all(sent, AXES, 0, 0)]
    ppermute x1, starting transfers between devices: 2.44 us -> 0.99 us  [local(): far = lax.ppermute(mine, ('c', 'x'), ring)]
  transfers between devices with their start and end apart: 4 -> 5, of which waited for: 1 -> 2; matrix products, arithmetic and copies ran while one was open for 0% -> 0% of each run, Pallas kernels for 27% -> 31%
where the time goes in v5:
time: 77.8 us; the launch traced here: 77.4 us
  Pallas kernels  32.5 us (42%)
  starting transfers between devices  19.2 us (25%)
  blocking collectives  14.2 us (18%)
  waiting for transfers between devices  10.8 us (14%)
    pallas_call x4, Pallas kernels, local(): pl.pallas_call(functools.partial(logits_kernel, part), in_specs=[VMEM] *...  19.8 us
    all_to_all x1, blocking collectives, local(): mine = lax.all_to_all(packed, ('z', 'y'), 0, 0)  14.2 us
    all_to_all x1, starting transfers between devices, local(): rotated = lax.all_to_all(sent, AXES, 0, 0)  11.5 us
    all_to_all x1, waiting for transfers between devices, local(): rotated = lax.all_to_all(sent, AXES, 0, 0)  5.82 us
    all_to_all x1, waiting for transfers between devices, local(): every = lax.all_to_all(wide[0], AXES, 0, 0)  4.94 us
    pallas_call x1, Pallas kernels, local(): pl.pallas_call(turn_kernel, grid=(n // block,), in_specs=[SMEM, rows], ou...  4.89 us
    pallas_call x1, Pallas kernels, local(): pl.pallas_call(norms_kernel, grid=(n // block,), in_specs=[rows], out_spe...  4.66 us
    all_to_all x1, starting transfers between devices, local(): every = lax.all_to_all(wide[0], AXES, 0, 0)  4.43 us
  transfers between devices with their start and end apart: 5, of which 2 were waited for; matrix products, arithmetic and copies ran while one was open for 0% of the time, Pallas kernels for 31%

profile of v5, /device:TPU:1, one launch (start us, length us, event | category | flops | bytes accessed | tf_op | source)
XLA Modules:
  0.0 77.4 jit_solution(7672950084780630052)
XLA Ops:
  0.0 1.7 %rotate.1 = f32[128,4,128]{2,1,0:T(4,128)} custom-call(s32[4]{0:T(128)} %pos_hbm.1, bf16[4,8192]{1,0:T(4,128)(2,1)} %q_hbm.1), custom_call_target="tpu_custom_call" | custom-call | tf_op jit(solution)/shard_map/rotate/pallas_call | solution.py:236
  1.7 11.5 %all-to-all-start = ((f32[128,4,128]{2,1,0:T(4,128)}), f32[128,4,128]{2,1,0:T(4,128)S(1)}, u32[]{:S(2)}, u32[]{:S(2)}) async-start(f32[128,4,128]{2,1,0:T(4,128)} %rotate.1), calls=%async_computation | async-start | bytes 524288 | tf_op jit(solution)/shard_map/all_to_all | solution.py:249
  13.8 4.9 %turn.1 = (bf16[128,4096]{1,0:T(8,128)(2,1)S(1)}, bf16[128,4096]{1,0:T(8,128)(2,1)S(1)}, bf16[128,4096]{1,0:T(8,128)(2,1)}, bf16[128,4096]{1,0:T(8,128)(2,1)}, s32[8,128]{1,0:T(8,128)S(1)}) custom-call(s32[1]{0:T(128)S(6)} %copy.7.len_ref, bf16[4096,512]{1,0:T(8,128)(2,1)} %k_ref.1), custom_call_target="tpu_custom_call" | custom-call | flops 2147483648 | bytes 8388608 | tf_op jit(solution)/shard_map/turn/pallas_call | solution.py:253
  18.7 5.8 %all-to-all-done.r_ref = f32[128,4,128]{2,1,0:T(4,128)S(1)} async-done(((f32[128,4,128]{2,1,0:T(4,128)}), f32[128,4,128]{2,1,0:T(4,128)S(1)}, u32[]{:S(2)}, u32[]{:S(2)}) %all-to-all-start) | async-done | bytes 262176 | tf_op jit(solution)/shard_map/all_to_all | solution.py:249
  24.5 0.5 stats.1
  25.1 14.2 %all_to_all.22.p_ref = f32[16,72,128]{2,1,0:T(8,128)S(1)} all-to-all(f32[16,72,128]{2,1,0:T(8,128)S(1)} %stats.1), channel_id=1, replica_groups=mesh['z'=4,'y'=4,'c'=2,'x'=4] {'z','y'}, dimensions={0} | all-to-all | bytes 1179648 | tf_op jit(solution)/shard_map/all_to_all | solution.py:275
  39.2 1.8 %collective-permute-start.1 = (f32[16,72,128]{2,1,0:T(8,128)S(1)}, f32[16,72,128]{2,1,0:T(8,128)S(1)}, u32[]{:S(2)}, u32[]{:S(2)}) collective-permute-start(f32[16,72,128]{2,1,0:T(8,128)S(1)} %all_to_all.22.p_ref), channel_id=1, source_target_pairs={{0,4},{4,0},{1,5},{5,1},{2,6},{6,2},{3,7},{7,3},{8,12},{12,8},{9,1... | collective-permute-start | bytes 1769480 | tf_op jit(solution)/shard_map/ppermute | solution.py:277
  41.0 1.0 %collective-permute-start = (f32[16,72,128]{2,1,0:T(8,128)S(1)}, f32[16,72,128]{2,1,0:T(8,128)S(1)}, u32[]{:S(2)}, u32[]{:S(2)}) collective-permute-start(f32[16,72,128]{2,1,0:T(8,128)S(1)} %all_to_all.22.p_ref), channel_id=1, source_target_pairs={{0,1},{1,2},{2,3},{3,0},{4,7},{5,4},{6,5},{7,6},{8,9},{9,10},{10,1... | collective-permute-start | bytes 1769480 | tf_op jit(solution)/shard_map/ppermute | solution.py:276
  42.0 4.8 %logits.4 = (f32[16,4096]{1,0:T(8,128)S(1)}, f32[8,128]{1,0:T(8,128)S(1)}) custom-call(s32[8,128]{1,0:T(8,128)S(1)} %get-tuple-element.34.live_ref, f32[16,72,128]{2,1,0:T(8,128)S(1)} %all_to_all.22.p_ref, bf16[128,4096]{1,0:T(8,128)(2,1)S(1)} %get-tuple-element.37.kt_ref), custom_call_target="tpu_custom_call" | custom-call | flops 2147483648 | bytes 2097152 | tf_op jit(solution)/shard_map/logits/pallas_call | solution.py:282
  46.8 0.0 copy-start.1
  46.8 0.0 collective-permute-done.1.p_ref
  46.8 4.8 %logits.5 = (f32[16,4096]{1,0:T(8,128)S(1)}, f32[8,128]{1,0:T(8,128)S(1)}) custom-call(s32[8,128]{1,0:T(8,128)S(1)} %get-tuple-element.34.live_ref, f32[16,72,128]{2,1,0:T(8,128)S(1)} %collective-permute-done.1.p_ref, bf16[128,4096]{1,0:T(8,128)(2,1)S(1)} %get-tuple-element.36.kt_ref, f32[8,128]{1,0:T(8,128)S(1)} %get-tuple-element.38.refs_0_), custom_call_target="tpu_custom_call" | custom-call | flops 2147483648 | bytes 2097152 | tf_op jit(solution)/shard_map/logits/pallas_call | solution.py:282
  51.6 0.0 copy-start
  51.6 0.0 collective-permute-done.p_ref
  51.6 0.5 collective-permute-start.2
  52.1 0.0 copy-done.1
  52.1 4.8 %logits.6 = (f32[16,4096]{1,0:T(8,128)S(1)}, f32[8,128]{1,0:T(8,128)S(1)}) custom-call(s32[8,128]{1,0:T(8,128)S(1)} %get-tuple-element.34.live_ref, f32[16,72,128]{2,1,0:T(8,128)S(1)} %collective-permute-done.p_ref, bf16[128,4096]{1,0:T(8,128)(2,1)S(1)} %copy-done.1, f32[8,128]{1,0:T(8,128)S(1)} %get-tuple-element.43.refs_0_), custom_call_target="tpu_custom_call" | custom-call | flops 2147483648 | bytes 2097152 | tf_op jit(solution)/shard_map/logits/pallas_call | solution.py:282
  56.9 0.0 collective-permute-done.2.p_ref
  56.9 0.0 copy-done
  56.9 5.4 %logits.7 = (f32[16,4096]{1,0:T(8,128)S(1)}, f32[8,128]{1,0:T(8,128)S(1)}, f32[128,128]{1,0:T(8,128)}) custom-call(s32[8,128]{1,0:T(8,128)S(1)} %get-tuple-element.34.live_ref, f32[16,72,128]{2,1,0:T(8,128)S(1)} %collective-permute-done.2.p_ref, bf16[128,4096]{1,0:T(8,128)(2,1)S(1)} %copy-done, f32[8,128]{1,0:T(8,128)S(1)} %get-tuple-element.44.refs_0_), custom_call_target="tpu_custom_call" | custom-call | flops 2147483648 | bytes 2097152 | tf_op jit(solution)/shard_map/logits/pallas_call | solution.py:282
  62.3 4.4 %all-to-all-start.2 = ((f32[128,1,128]{2,1,0:T(1,128)}), f32[128,1,128]{2,1,0:T(1,128)S(1)}, u32[]{:S(2)}, u32[]{:S(2)}) async-start(f32[128,1,128]{2,1,0:T(1,128)} %bitcast.1), calls=%async_computation.2 | async-start | bytes 131072 | tf_op jit(solution)/shard_map/all_to_all | solution.py:304
  66.7 4.7 %norms.1.refs_4_ = f32[4,4096]{1,0:T(4,128)S(1)} custom-call(bf16[4096,512]{1,0:T(8,128)(2,1)} %v_ref.1), custom_call_target="tpu_custom_call" | custom-call | flops 2147483648 | bytes 4194304 | tf_op jit(solution)/shard_map/norms/pallas_call | solution.py:305
  71.4 4.9 %all-to-all-done.2 = f32[128,1,128]{2,1,0:T(1,128)S(1)} async-done(((f32[128,1,128]{2,1,0:T(1,128)}), f32[128,1,128]{2,1,0:T(1,128)S(1)}, u32[]{:S(2)}, u32[]{:S(2)}) %all-to-all-start.2) | async-done | bytes 65568 | tf_op jit(solution)/shard_map/all_to_all | solution.py:304
  76.3 1.0 %scores.1 = f32[4,4096]{1,0:T(4,128)} custom-call(f32[128,128]{1,0:T(8,128)S(1)} %bitcast.4, f32[8,128]{1,0:T(8,128)S(1)} %get-tuple-element.47.mine_ref, f32[16,4096]{1,0:T(8,128)S(1)} %get-tuple-element.48.refs_0_, f32[16,4096]{1,0:T(8,128)S(1)} %get-tuple-element.49.refs_1_, f32[16,4096]{1,0:T(8,128)S(1)} %get-tuple-element.50.refs_2_, ...), custom_call_target="tpu_custom_call" | custom-call | tf_op jit(solution)/shard_map/scores/pallas_call | solution.py:317
Async XLA Ops:
  1.7 22.9 %all-to-all-start = ((f32[128,4,128]{2,1,0:T(4,128)}), f32[128,4,128]{2,1,0:T(4,128)S(1)}, u32[]{:S(2)}, u32[]{:S(2)}) async-start(f32[128,4,128]{2,1,0:T(4,128)} %rotate.1), calls=%async_computation | async-start | bytes 524288 | tf_op jit(solution)/shard_map/all_to_all | solution.py:249
  39.2 7.6 %collective-permute-start.1 = (f32[16,72,128]{2,1,0:T(8,128)S(1)}, f32[16,72,128]{2,1,0:T(8,128)S(1)}, u32[]{:S(2)}, u32[]{:S(2)}) collective-permute-start(f32[16,72,128]{2,1,0:T(8,128)S(1)} %all_to_all.22.p_ref), channel_id=1, source_target_pairs={{0,4},{4,0},{1,5},{5,1},{2,6},{6,2},{3,7},{7,3},{8,12},{12,8},{9,1... | collective-permute-start | bytes 1769480 | tf_op jit(solution)/shard_map/ppermute | solution.py:277
  41.0 10.6 %collective-permute-start = (f32[16,72,128]{2,1,0:T(8,128)S(1)}, f32[16,72,128]{2,1,0:T(8,128)S(1)}, u32[]{:S(2)}, u32[]{:S(2)}) collective-permute-start(f32[16,72,128]{2,1,0:T(8,128)S(1)} %all_to_all.22.p_ref), channel_id=1, source_target_pairs={{0,1},{1,2},{2,3},{3,0},{4,7},{5,4},{6,5},{7,6},{8,9},{9,10},{10,1... | collective-permute-start | bytes 1769480 | tf_op jit(solution)/shard_map/ppermute | solution.py:276
  46.8 5.3 %copy-start.1 = (bf16[128,4096]{1,0:T(8,128)(2,1)S(1)}, bf16[128,4096]{1,0:T(8,128)(2,1)}, u32[]{:S(2)}) copy-start(bf16[128,4096]{1,0:T(8,128)(2,1)} %get-tuple-element.42.kt_ref) | copy-start | bytes 3145732
  51.6 5.3 %copy-start = (bf16[128,4096]{1,0:T(8,128)(2,1)S(1)}, bf16[128,4096]{1,0:T(8,128)(2,1)}, u32[]{:S(2)}) copy-start(bf16[128,4096]{1,0:T(8,128)(2,1)} %get-tuple-element.41.kt_ref) | copy-start | bytes 3145732
  51.6 5.3 %collective-permute-start.2 = (f32[16,72,128]{2,1,0:T(8,128)S(1)}, f32[16,72,128]{2,1,0:T(8,128)S(1)}, u32[]{:S(2)}, u32[]{:S(2)}) collective-permute-start(f32[16,72,128]{2,1,0:T(8,128)S(1)} %collective-permute-done.p_ref), channel_id=1, source_target_pairs={{0,4},{4,0},{1,5},{5,1},{2,6},{6,2},{3,7},{7,3},{8,12},{12,8},{9,1... | collective-permute-start | bytes 1769480 | tf_op jit(solution)/shard_map/ppermute | solution.py:302
  62.3 14.1 %all-to-all-start.2 = ((f32[128,1,128]{2,1,0:T(1,128)}), f32[128,1,128]{2,1,0:T(1,128)S(1)}, u32[]{:S(2)}, u32[]{:S(2)}) async-start(f32[128,1,128]{2,1,0:T(1,128)} %bitcast.1), calls=%async_computation.2 | async-start | bytes 131072 | tf_op jit(solution)/shard_map/all_to_all | solution.py:304

commit v6 on v5

--- a/solution.py
+++ b/solution.py
@@ -250,11 +250,12 @@
 
     block = 1024
     rows = pl.BlockSpec((block, KVH * HD), lambda i: (i, 0))
+    part = 2048
     *keys_t, live = pl.pallas_call(
         turn_kernel,
-        grid=(n // block,),
-        in_specs=[SMEM, rows],
-        out_specs=[pl.BlockSpec((HD, block), lambda i: (0, i))] * KVH + [pl.BlockSpec((8, HD), lambda i: (0, 0))],
+        grid=(n // part,),
+        in_specs=[SMEM, pl.BlockSpec((part, KVH * HD), lambda i: (i, 0))],
+        out_specs=[pl.BlockSpec((HD, part), lambda i: (0, i))] * KVH + [pl.BlockSpec((8, HD), lambda i: (0, 0))],
         out_shape=[jax.ShapeDtypeStruct((HD, n), BF16)] * KVH + [jax.ShapeDtypeStruct((8, HD), jnp.int32)],
         compiler_params=params(51),
         cost_estimate=pl.CostEstimate(flops=2 * n * 512 * 512, bytes_accessed=8 * 2**20, transcendentals=0),

time: 77.8 us -> 77.7 us (level)
  Pallas kernels: 32.5 us -> 31.5 us
  waiting for transfers between devices: 10.8 us -> 11.8 us
    all_to_all x1, waiting for transfers between devices: 5.82 us -> 6.81 us  [local(): rotated = lax.all_to_all(sent, AXES, 0, 0)]
    pallas_call x1, Pallas kernels: 4.89 us -> 3.9 us  [local(): pl.pallas_call(turn_kernel, grid=(n // part,), in_specs=[SMEM, pl.BlockSp...]
  transfers between devices with their start and end apart: 5 -> 5, of which waited for: 2 -> 2; matrix products, arithmetic and copies ran while one was open for 0% -> 0% of each run, Pallas kernels for 31% -> 30%
where the time goes in v6:
time: 77.7 us; the launch traced here: 77.4 us
  Pallas kernels  31.5 us (41%)
  starting transfers between devices  19.2 us (25%)
  blocking collectives  14.2 us (18%)
  waiting for transfers between devices  11.8 us (15%)
    pallas_call x4, Pallas kernels, local(): pl.pallas_call(functools.partial(logits_kernel, part), in_specs=[VMEM] *...  19.8 us
    all_to_all x1, blocking collectives, local(): mine = lax.all_to_all(packed, ('z', 'y'), 0, 0)  14.2 us
    all_to_all x1, starting transfers between devices, local(): rotated = lax.all_to_all(sent, AXES, 0, 0)  11.5 us
    all_to_all x1, waiting for transfers between devices, local(): rotated = lax.all_to_all(sent, AXES, 0, 0)  6.81 us
    all_to_all x1, waiting for transfers between devices, local(): every = lax.all_to_all(wide[0], AXES, 0, 0)  4.94 us
    pallas_call x1, Pallas kernels, local(): pl.pallas_call(norms_kernel, grid=(n // block,), in_specs=[rows], out_spe...  4.66 us
    all_to_all x1, starting transfers between devices, local(): every = lax.all_to_all(wide[0], AXES, 0, 0)  4.43 us
    pallas_call x1, Pallas kernels, local(): pl.pallas_call(turn_kernel, grid=(n // part,), in_specs=[SMEM, pl.BlockSp...  3.9 us
  transfers between devices with their start and end apart: 5, of which 2 were waited for; matrix products, arithmetic and copies ran while one was open for 0% of the time, Pallas kernels for 30%

profile of v6, /device:TPU:1, one launch (start us, length us, event | category | flops | bytes accessed | tf_op | source)
XLA Modules:
  0.0 77.4 jit_solution(10282334461712295918)
XLA Ops:
  0.0 1.7 %rotate.1 = f32[128,4,128]{2,1,0:T(4,128)} custom-call(s32[4]{0:T(128)} %pos_hbm.1, bf16[4,8192]{1,0:T(4,128)(2,1)} %q_hbm.1), custom_call_target="tpu_custom_call" | custom-call | tf_op jit(solution)/shard_map/rotate/pallas_call | solution.py:236
  1.7 11.5 %all-to-all-start = ((f32[128,4,128]{2,1,0:T(4,128)}), f32[128,4,128]{2,1,0:T(4,128)S(1)}, u32[]{:S(2)}, u32[]{:S(2)}) async-start(f32[128,4,128]{2,1,0:T(4,128)} %rotate.1), calls=%async_computation | async-start | bytes 524288 | tf_op jit(solution)/shard_map/all_to_all | solution.py:249
  13.8 3.9 %turn.1 = (bf16[128,4096]{1,0:T(8,128)(2,1)S(1)}, bf16[128,4096]{1,0:T(8,128)(2,1)S(1)}, bf16[128,4096]{1,0:T(8,128)(2,1)}, bf16[128,4096]{1,0:T(8,128)(2,1)}, s32[8,128]{1,0:T(8,128)S(1)}) custom-call(s32[1]{0:T(128)S(6)} %copy.7.len_ref, bf16[4096,512]{1,0:T(8,128)(2,1)} %k_ref.1), custom_call_target="tpu_custom_call" | custom-call | flops 2147483648 | bytes 8388608 | tf_op jit(solution)/shard_map/turn/pallas_call | solution.py:254
  17.7 6.8 %all-to-all-done.r_ref = f32[128,4,128]{2,1,0:T(4,128)S(1)} async-done(((f32[128,4,128]{2,1,0:T(4,128)}), f32[128,4,128]{2,1,0:T(4,128)S(1)}, u32[]{:S(2)}, u32[]{:S(2)}) %all-to-all-start) | async-done | bytes 262176 | tf_op jit(solution)/shard_map/all_to_all | solution.py:249
  24.5 0.5 stats.1
  25.1 14.2 %all_to_all.22.p_ref = f32[16,72,128]{2,1,0:T(8,128)S(1)} all-to-all(f32[16,72,128]{2,1,0:T(8,128)S(1)} %stats.1), channel_id=1, replica_groups=mesh['z'=4,'y'=4,'c'=2,'x'=4] {'z','y'}, dimensions={0} | all-to-all | bytes 1179648 | tf_op jit(solution)/shard_map/all_to_all | solution.py:276
  39.2 1.8 %collective-permute-start.1 = (f32[16,72,128]{2,1,0:T(8,128)S(1)}, f32[16,72,128]{2,1,0:T(8,128)S(1)}, u32[]{:S(2)}, u32[]{:S(2)}) collective-permute-start(f32[16,72,128]{2,1,0:T(8,128)S(1)} %all_to_all.22.p_ref), channel_id=1, source_target_pairs={{0,4},{4,0},{1,5},{5,1},{2,6},{6,2},{3,7},{7,3},{8,12},{12,8},{9,1... | collective-permute-start | bytes 1769480 | tf_op jit(solution)/shard_map/ppermute | solution.py:278
  41.0 1.0 %collective-permute-start = (f32[16,72,128]{2,1,0:T(8,128)S(1)}, f32[16,72,128]{2,1,0:T(8,128)S(1)}, u32[]{:S(2)}, u32[]{:S(2)}) collective-permute-start(f32[16,72,128]{2,1,0:T(8,128)S(1)} %all_to_all.22.p_ref), channel_id=1, source_target_pairs={{0,1},{1,2},{2,3},{3,0},{4,7},{5,4},{6,5},{7,6},{8,9},{9,10},{10,1... | collective-permute-start | bytes 1769480 | tf_op jit(solution)/shard_map/ppermute | solution.py:277
  42.0 4.8 %logits.4 = (f32[16,4096]{1,0:T(8,128)S(1)}, f32[8,128]{1,0:T(8,128)S(1)}) custom-call(s32[8,128]{1,0:T(8,128)S(1)} %get-tuple-element.34.live_ref, f32[16,72,128]{2,1,0:T(8,128)S(1)} %all_to_all.22.p_ref, bf16[128,4096]{1,0:T(8,128)(2,1)S(1)} %get-tuple-element.37.kt_ref), custom_call_target="tpu_custom_call" | custom-call | flops 2147483648 | bytes 2097152 | tf_op jit(solution)/shard_map/logits/pallas_call | solution.py:283
  46.8 0.0 copy-start.1
  46.8 0.0 collective-permute-done.1.p_ref
  46.8 4.8 %logits.5 = (f32[16,4096]{1,0:T(8,128)S(1)}, f32[8,128]{1,0:T(8,128)S(1)}) custom-call(s32[8,128]{1,0:T(8,128)S(1)} %get-tuple-element.34.live_ref, f32[16,72,128]{2,1,0:T(8,128)S(1)} %collective-permute-done.1.p_ref, bf16[128,4096]{1,0:T(8,128)(2,1)S(1)} %get-tuple-element.36.kt_ref, f32[8,128]{1,0:T(8,128)S(1)} %get-tuple-element.38.refs_0_), custom_call_target="tpu_custom_call" | custom-call | flops 2147483648 | bytes 2097152 | tf_op jit(solution)/shard_map/logits/pallas_call | solution.py:283
  51.6 0.0 copy-start
  51.6 0.0 collective-permute-done.p_ref
  51.6 0.5 collective-permute-start.2
  52.1 0.0 copy-done.1
  52.1 4.8 %logits.6 = (f32[16,4096]{1,0:T(8,128)S(1)}, f32[8,128]{1,0:T(8,128)S(1)}) custom-call(s32[8,128]{1,0:T(8,128)S(1)} %get-tuple-element.34.live_ref, f32[16,72,128]{2,1,0:T(8,128)S(1)} %collective-permute-done.p_ref, bf16[128,4096]{1,0:T(8,128)(2,1)S(1)} %copy-done.1, f32[8,128]{1,0:T(8,128)S(1)} %get-tuple-element.43.refs_0_), custom_call_target="tpu_custom_call" | custom-call | flops 2147483648 | bytes 2097152 | tf_op jit(solution)/shard_map/logits/pallas_call | solution.py:283
  56.9 0.0 collective-permute-done.2.p_ref
  56.9 0.0 copy-done
  56.9 5.4 %logits.7 = (f32[16,4096]{1,0:T(8,128)S(1)}, f32[8,128]{1,0:T(8,128)S(1)}, f32[128,128]{1,0:T(8,128)}) custom-call(s32[8,128]{1,0:T(8,128)S(1)} %get-tuple-element.34.live_ref, f32[16,72,128]{2,1,0:T(8,128)S(1)} %collective-permute-done.2.p_ref, bf16[128,4096]{1,0:T(8,128)(2,1)S(1)} %copy-done, f32[8,128]{1,0:T(8,128)S(1)} %get-tuple-element.44.refs_0_), custom_call_target="tpu_custom_call" | custom-call | flops 2147483648 | bytes 2097152 | tf_op jit(solution)/shard_map/logits/pallas_call | solution.py:283
  62.3 4.4 %all-to-all-start.2 = ((f32[128,1,128]{2,1,0:T(1,128)}), f32[128,1,128]{2,1,0:T(1,128)S(1)}, u32[]{:S(2)}, u32[]{:S(2)}) async-start(f32[128,1,128]{2,1,0:T(1,128)} %bitcast.1), calls=%async_computation.2 | async-start | bytes 131072 | tf_op jit(solution)/shard_map/all_to_all | solution.py:305
  66.7 4.7 %norms.1.refs_4_ = f32[4,4096]{1,0:T(4,128)S(1)} custom-call(bf16[4096,512]{1,0:T(8,128)(2,1)} %v_ref.1), custom_call_target="tpu_custom_call" | custom-call | flops 2147483648 | bytes 4194304 | tf_op jit(solution)/shard_map/norms/pallas_call | solution.py:306
  71.4 4.9 %all-to-all-done.2 = f32[128,1,128]{2,1,0:T(1,128)S(1)} async-done(((f32[128,1,128]{2,1,0:T(1,128)}), f32[128,1,128]{2,1,0:T(1,128)S(1)}, u32[]{:S(2)}, u32[]{:S(2)}) %all-to-all-start.2) | async-done | bytes 65568 | tf_op jit(solution)/shard_map/all_to_all | solution.py:305
  76.3 1.0 %scores.1 = f32[4,4096]{1,0:T(4,128)} custom-call(f32[128,128]{1,0:T(8,128)S(1)} %bitcast.4, f32[8,128]{1,0:T(8,128)S(1)} %get-tuple-element.47.mine_ref, f32[16,4096]{1,0:T(8,128)S(1)} %get-tuple-element.48.refs_0_, f32[16,4096]{1,0:T(8,128)S(1)} %get-tuple-element.49.refs_1_, f32[16,4096]{1,0:T(8,128)S(1)} %get-tuple-element.50.refs_2_, ...), custom_call_target="tpu_custom_call" | custom-call | tf_op jit(solution)/shard_map/scores/pallas_call | solution.py:318
Async XLA Ops:
  1.7 22.9 %all-to-all-start = ((f32[128,4,128]{2,1,0:T(4,128)}), f32[128,4,128]{2,1,0:T(4,128)S(1)}, u32[]{:S(2)}, u32[]{:S(2)}) async-start(f32[128,4,128]{2,1,0:T(4,128)} %rotate.1), calls=%async_computation | async-start | bytes 524288 | tf_op jit(solution)/shard_map/all_to_all | solution.py:249
  39.2 7.6 %collective-permute-start.1 = (f32[16,72,128]{2,1,0:T(8,128)S(1)}, f32[16,72,128]{2,1,0:T(8,128)S(1)}, u32[]{:S(2)}, u32[]{:S(2)}) collective-permute-start(f32[16,72,128]{2,1,0:T(8,128)S(1)} %all_to_all.22.p_ref), channel_id=1, source_target_pairs={{0,4},{4,0},{1,5},{5,1},{2,6},{6,2},{3,7},{7,3},{8,12},{12,8},{9,1... | collective-permute-start | bytes 1769480 | tf_op jit(solution)/shard_map/ppermute | solution.py:278
  41.0 10.6 %collective-permute-start = (f32[16,72,128]{2,1,0:T(8,128)S(1)}, f32[16,72,128]{2,1,0:T(8,128)S(1)}, u32[]{:S(2)}, u32[]{:S(2)}) collective-permute-start(f32[16,72,128]{2,1,0:T(8,128)S(1)} %all_to_all.22.p_ref), channel_id=1, source_target_pairs={{0,1},{1,2},{2,3},{3,0},{4,7},{5,4},{6,5},{7,6},{8,9},{9,10},{10,1... | collective-permute-start | bytes 1769480 | tf_op jit(solution)/shard_map/ppermute | solution.py:277
  46.8 5.3 %copy-start.1 = (bf16[128,4096]{1,0:T(8,128)(2,1)S(1)}, bf16[128,4096]{1,0:T(8,128)(2,1)}, u32[]{:S(2)}) copy-start(bf16[128,4096]{1,0:T(8,128)(2,1)} %get-tuple-element.42.kt_ref) | copy-start | bytes 3145732
  51.6 5.3 %copy-start = (bf16[128,4096]{1,0:T(8,128)(2,1)S(1)}, bf16[128,4096]{1,0:T(8,128)(2,1)}, u32[]{:S(2)}) copy-start(bf16[128,4096]{1,0:T(8,128)(2,1)} %get-tuple-element.41.kt_ref) | copy-start | bytes 3145732
  51.6 5.3 %collective-permute-start.2 = (f32[16,72,128]{2,1,0:T(8,128)S(1)}, f32[16,72,128]{2,1,0:T(8,128)S(1)}, u32[]{:S(2)}, u32[]{:S(2)}) collective-permute-start(f32[16,72,128]{2,1,0:T(8,128)S(1)} %collective-permute-done.p_ref), channel_id=1, source_target_pairs={{0,4},{4,0},{1,5},{5,1},{2,6},{6,2},{3,7},{7,3},{8,12},{12,8},{9,1... | collective-permute-start | bytes 1769480 | tf_op jit(solution)/shard_map/ppermute | solution.py:303
  62.3 14.1 %all-to-all-start.2 = ((f32[128,1,128]{2,1,0:T(1,128)}), f32[128,1,128]{2,1,0:T(1,128)S(1)}, u32[]{:S(2)}, u32[]{:S(2)}) async-start(f32[128,1,128]{2,1,0:T(1,128)} %bitcast.1), calls=%async_computation.2 | async-start | bytes 131072 | tf_op jit(solution)/shard_map/all_to_all | solution.py:305

commit v7 on v6

--- a/solution.py
+++ b/solution.py
@@ -95,10 +95,7 @@
     return (1 - chunk if far else chunk), (1 - side if other else side)
 
 
-def turn_kernel(len_ref, k_ref, *refs):
-    kt_refs, live_ref = refs[:-1], refs[-1]
-    here = pl.num_programs(0) * k_ref.shape[0]
-    live_ref[...] = jnp.full(live_ref.shape, len_ref[0] - lax.axis_index(AXES) * here, jnp.int32)
+def turn_kernel(k_ref, *kt_refs):
     for part, kt_ref in zip(PARTS, kt_refs):
         chunk, side = place(*part)
         low, high = k_ref[:, : CHUNKS * HD], k_ref[:, CHUNKS * HD :]
@@ -183,7 +180,8 @@
         quad = jnp.concatenate(quad, axis=0) + corner_sum(corner_ref, kf)
         w_out[:, s : s + step] = quad * (0.5 / HD) + lin * (1.0 / math.sqrt(HD))
     lg = w_out[...]
-    live = iota(lg.shape, 1) < jnp.broadcast_to(live_ref[0:1, 0:1], lg.shape)
+    start = lax.axis_index(AXES) * width
+    live = start + iota(lg.shape, 1) < jnp.broadcast_to(live_ref[...], lg.shape)
     peak = jnp.max(jnp.where(live, lg, -1e30), axis=1, keepdims=True)
     w = jnp.where(live, jnp.exp(jnp.where(live, lg - peak, 0.0)), 0.0)
     w_out[...] = w
@@ -251,17 +249,17 @@
     block = 1024
     rows = pl.BlockSpec((block, KVH * HD), lambda i: (i, 0))
     part = 2048
-    *keys_t, live = pl.pallas_call(
+    keys_t = pl.pallas_call(
         turn_kernel,
         grid=(n // part,),
-        in_specs=[SMEM, pl.BlockSpec((part, KVH * HD), lambda i: (i, 0))],
-        out_specs=[pl.BlockSpec((HD, part), lambda i: (0, i))] * KVH + [pl.BlockSpec((8, HD), lambda i: (0, 0))],
-        out_shape=[jax.ShapeDtypeStruct((HD, n), BF16)] * KVH + [jax.ShapeDtypeStruct((8, HD), jnp.int32)],
+        in_specs=[pl.BlockSpec((part, KVH * HD), lambda i: (i, 0))],
+        out_specs=[pl.BlockSpec((HD, part), lambda i: (0, i))] * KVH,
+        out_shape=[jax.ShapeDtypeStruct((HD, n), BF16)] * KVH,
         compiler_params=params(51),
         cost_estimate=pl.CostEstimate(flops=2 * n * 512 * 512, bytes_accessed=8 * 2**20, transcendentals=0),
         name="turn",
-    )(cache_length, keys)
-    rotated, keys_t, live = lax.optimization_barrier((rotated, keys_t, live))
+    )(keys)
+    rotated, keys_t = lax.optimization_barrier((rotated, keys_t))
 
     packed = pl.pallas_call(
         stats_kernel,
@@ -296,7 +294,7 @@
                 flops=2 * n * GROUP * HD * HD, bytes_accessed=2 * 2**20, transcendentals=n * GROUP
             ),
             name="logits",
-        )(live, stats[i], keys_t[i], *st)
+        )(cache_length.reshape(1, 1), stats[i], keys_t[i], *st)
         weights.append(w)
         if i == NC - 1:
             far, now = lax.optimization_barrier((far, now))

time: 77.7 us -> 78.2 us (level)
  transfers between devices with their start and end apart: 5 -> 5, of which waited for: 2 -> 2; matrix products, arithmetic and copies ran while one was open for 0% -> 0% of each run, Pallas kernels for 30% -> 29%
where the time goes in v7:
time: 78.2 us; the launch traced here: 77.9 us
  Pallas kernels  31.4 us (40%)
  starting transfers between devices  19.1 us (24%)
  blocking collectives  14.2 us (18%)
  waiting for transfers between devices  12.4 us (16%)
    pallas_call x4, Pallas kernels, local(): pl.pallas_call(functools.partial(logits_kernel, part), in_specs=[VMEM] *...  19.7 us
    all_to_all x1, blocking collectives, local(): mine = lax.all_to_all(packed, ('z', 'y'), 0, 0)  14.2 us
    all_to_all x1, starting transfers between devices, local(): rotated = lax.all_to_all(sent, AXES, 0, 0)  11.5 us
    all_to_all x1, waiting for transfers between devices, local(): rotated = lax.all_to_all(sent, AXES, 0, 0)  7.46 us
    all_to_all x1, waiting for transfers between devices, local(): every = lax.all_to_all(wide[0], AXES, 0, 0)  4.94 us
    pallas_call x1, Pallas kernels, local(): pl.pallas_call(norms_kernel, grid=(n // block,), in_specs=[rows], out_spe...  4.66 us
    all_to_all x1, starting transfers between devices, local(): every = lax.all_to_all(wide[0], AXES, 0, 0)  4.58 us
    pallas_call x1, Pallas kernels, local(): pl.pallas_call(turn_kernel, grid=(n // part,), in_specs=[pl.BlockSpec((pa...  3.89 us
  transfers between devices with their start and end apart: 5, of which 2 were waited for; matrix products, arithmetic and copies ran while one was open for 0% of the time, Pallas kernels for 29%

profile of v7, /device:TPU:1, one launch (start us, length us, event | category | flops | bytes accessed | tf_op | source)
XLA Modules:
  0.0 77.9 jit_solution(14872634343175757160)
XLA Ops:
  0.0 1.7 %rotate.1 = f32[128,4,128]{2,1,0:T(4,128)} custom-call(s32[4]{0:T(128)} %pos_hbm.1, bf16[4,8192]{1,0:T(4,128)(2,1)} %q_hbm.1), custom_call_target="tpu_custom_call" | custom-call | tf_op jit(solution)/shard_map/rotate/pallas_call | solution.py:234
  1.7 11.5 %all-to-all-start = ((f32[128,4,128]{2,1,0:T(4,128)}), f32[128,4,128]{2,1,0:T(4,128)S(1)}, u32[]{:S(2)}, u32[]{:S(2)}) async-start(f32[128,4,128]{2,1,0:T(4,128)} %rotate.1), calls=%async_computation | async-start | bytes 524288 | tf_op jit(solution)/shard_map/all_to_all | solution.py:247
  13.2 3.9 %turn.1 = (bf16[128,4096]{1,0:T(8,128)(2,1)S(1)}, bf16[128,4096]{1,0:T(8,128)(2,1)S(1)}, bf16[128,4096]{1,0:T(8,128)(2,1)}, bf16[128,4096]{1,0:T(8,128)(2,1)}) custom-call(bf16[4096,512]{1,0:T(8,128)(2,1)} %k_ref.1), custom_call_target="tpu_custom_call" | custom-call | flops 2147483648 | bytes 8388608 | tf_op jit(solution)/shard_map/turn/pallas_call | solution.py:252
  17.1 7.5 %all-to-all-done.r_ref = f32[128,4,128]{2,1,0:T(4,128)S(1)} async-done(((f32[128,4,128]{2,1,0:T(4,128)}), f32[128,4,128]{2,1,0:T(4,128)S(1)}, u32[]{:S(2)}, u32[]{:S(2)}) %all-to-all-start) | async-done | bytes 262176 | tf_op jit(solution)/shard_map/all_to_all | solution.py:247
  24.5 0.5 stats.1
  25.1 14.2 %all_to_all.22.p_ref = f32[16,72,128]{2,1,0:T(8,128)S(1)} all-to-all(f32[16,72,128]{2,1,0:T(8,128)S(1)} %stats.1), channel_id=1, replica_groups=mesh['z'=4,'y'=4,'c'=2,'x'=4] {'z','y'}, dimensions={0} | all-to-all | bytes 1179648 | tf_op jit(solution)/shard_map/all_to_all | solution.py:274
  39.2 1.8 %collective-permute-start.1 = (f32[16,72,128]{2,1,0:T(8,128)S(1)}, f32[16,72,128]{2,1,0:T(8,128)S(1)}, u32[]{:S(2)}, u32[]{:S(2)}) collective-permute-start(f32[16,72,128]{2,1,0:T(8,128)S(1)} %all_to_all.22.p_ref), channel_id=1, source_target_pairs={{0,4},{4,0},{1,5},{5,1},{2,6},{6,2},{3,7},{7,3},{8,12},{12,8},{9,1... | collective-permute-start | bytes 1769480 | tf_op jit(solution)/shard_map/ppermute | solution.py:276
  41.0 1.0 %collective-permute-start = (f32[16,72,128]{2,1,0:T(8,128)S(1)}, f32[16,72,128]{2,1,0:T(8,128)S(1)}, u32[]{:S(2)}, u32[]{:S(2)}) collective-permute-start(f32[16,72,128]{2,1,0:T(8,128)S(1)} %all_to_all.22.p_ref), channel_id=1, source_target_pairs={{0,1},{1,2},{2,3},{3,0},{4,7},{5,4},{6,5},{7,6},{8,9},{9,10},{10,1... | collective-permute-start | bytes 1769480 | tf_op jit(solution)/shard_map/ppermute | solution.py:275
  42.7 4.8 %logits.4 = (f32[16,4096]{1,0:T(8,128)S(1)}, f32[8,128]{1,0:T(8,128)S(1)}) custom-call(s32[1,1]{1,0:T(1,128)} %bitcast.5.live_ref, f32[16,72,128]{2,1,0:T(8,128)S(1)} %all_to_all.22.p_ref, bf16[128,4096]{1,0:T(8,128)(2,1)S(1)} %get-tuple-element.33.kt_ref), custom_call_target="tpu_custom_call" | custom-call | flops 2147483648 | bytes 2097152 | tf_op jit(solution)/shard_map/logits/pallas_call | solution.py:281
  47.4 0.0 copy-start.1
  47.4 0.0 collective-permute-done.1.p_ref
  47.4 4.8 %logits.5 = (f32[16,4096]{1,0:T(8,128)S(1)}, f32[8,128]{1,0:T(8,128)S(1)}) custom-call(s32[1,1]{1,0:T(1,128)} %bitcast.6.live_ref, f32[16,72,128]{2,1,0:T(8,128)S(1)} %collective-permute-done.1.p_ref, bf16[128,4096]{1,0:T(8,128)(2,1)S(1)} %get-tuple-element.32.kt_ref, f32[8,128]{1,0:T(8,128)S(1)} %get-tuple-element.34.refs_0_), custom_call_target="tpu_custom_call" | custom-call | flops 2147483648 | bytes 2097152 | tf_op jit(solution)/shard_map/logits/pallas_call | solution.py:281
  52.2 0.0 copy-start
  52.2 0.0 collective-permute-done.p_ref
  52.2 0.3 collective-permute-start.2
  52.5 0.0 copy-done.1
  52.5 4.8 %logits.6 = (f32[16,4096]{1,0:T(8,128)S(1)}, f32[8,128]{1,0:T(8,128)S(1)}) custom-call(s32[1,1]{1,0:T(1,128)} %bitcast.7.live_ref, f32[16,72,128]{2,1,0:T(8,128)S(1)} %collective-permute-done.p_ref, bf16[128,4096]{1,0:T(8,128)(2,1)S(1)} %copy-done.1, f32[8,128]{1,0:T(8,128)S(1)} %get-tuple-element.39.refs_0_), custom_call_target="tpu_custom_call" | custom-call | flops 2147483648 | bytes 2097152 | tf_op jit(solution)/shard_map/logits/pallas_call | solution.py:281
  57.3 0.0 collective-permute-done.2.p_ref
  57.3 0.0 copy-done
  57.3 5.4 %logits.7 = (f32[16,4096]{1,0:T(8,128)S(1)}, f32[8,128]{1,0:T(8,128)S(1)}, f32[128,128]{1,0:T(8,128)}) custom-call(s32[1,1]{1,0:T(1,128)} %bitcast.8.live_ref, f32[16,72,128]{2,1,0:T(8,128)S(1)} %collective-permute-done.2.p_ref, bf16[128,4096]{1,0:T(8,128)(2,1)S(1)} %copy-done, f32[8,128]{1,0:T(8,128)S(1)} %get-tuple-element.40.refs_0_), custom_call_target="tpu_custom_call" | custom-call | flops 2147483648 | bytes 2097152 | tf_op jit(solution)/shard_map/logits/pallas_call | solution.py:281
  62.7 4.6 %all-to-all-start.2 = ((f32[128,1,128]{2,1,0:T(1,128)}), f32[128,1,128]{2,1,0:T(1,128)S(1)}, u32[]{:S(2)}, u32[]{:S(2)}) async-start(f32[128,1,128]{2,1,0:T(1,128)} %bitcast.2), calls=%async_computation.2 | async-start | bytes 131072 | tf_op jit(solution)/shard_map/all_to_all | solution.py:303
  67.3 4.7 %norms.1.refs_4_ = f32[4,4096]{1,0:T(4,128)S(1)} custom-call(bf16[4096,512]{1,0:T(8,128)(2,1)} %v_ref.1), custom_call_target="tpu_custom_call" | custom-call | flops 2147483648 | bytes 4194304 | tf_op jit(solution)/shard_map/norms/pallas_call | solution.py:304
  71.9 4.9 %all-to-all-done.2 = f32[128,1,128]{2,1,0:T(1,128)S(1)} async-done(((f32[128,1,128]{2,1,0:T(1,128)}), f32[128,1,128]{2,1,0:T(1,128)S(1)}, u32[]{:S(2)}, u32[]{:S(2)}) %all-to-all-start.2) | async-done | bytes 65568 | tf_op jit(solution)/shard_map/all_to_all | solution.py:303
  76.9 1.0 %scores.1 = f32[4,4096]{1,0:T(4,128)} custom-call(f32[128,128]{1,0:T(8,128)S(1)} %bitcast.9, f32[8,128]{1,0:T(8,128)S(1)} %get-tuple-element.43.mine_ref, f32[16,4096]{1,0:T(8,128)S(1)} %get-tuple-element.44.refs_0_, f32[16,4096]{1,0:T(8,128)S(1)} %get-tuple-element.45.refs_1_, f32[16,4096]{1,0:T(8,128)S(1)} %get-tuple-element.46.refs_2_, ...), custom_call_target="tpu_custom_call" | custom-call | tf_op jit(solution)/shard_map/scores/pallas_call | solution.py:316
Async XLA Ops:
  1.7 22.9 %all-to-all-start = ((f32[128,4,128]{2,1,0:T(4,128)}), f32[128,4,128]{2,1,0:T(4,128)S(1)}, u32[]{:S(2)}, u32[]{:S(2)}) async-start(f32[128,4,128]{2,1,0:T(4,128)} %rotate.1), calls=%async_computation | async-start | bytes 524288 | tf_op jit(solution)/shard_map/all_to_all | solution.py:247
  39.2 8.2 %collective-permute-start.1 = (f32[16,72,128]{2,1,0:T(8,128)S(1)}, f32[16,72,128]{2,1,0:T(8,128)S(1)}, u32[]{:S(2)}, u32[]{:S(2)}) collective-permute-start(f32[16,72,128]{2,1,0:T(8,128)S(1)} %all_to_all.22.p_ref), channel_id=1, source_target_pairs={{0,4},{4,0},{1,5},{5,1},{2,6},{6,2},{3,7},{7,3},{8,12},{12,8},{9,1... | collective-permute-start | bytes 1769480 | tf_op jit(solution)/shard_map/ppermute | solution.py:276
  41.0 11.2 %collective-permute-start = (f32[16,72,128]{2,1,0:T(8,128)S(1)}, f32[16,72,128]{2,1,0:T(8,128)S(1)}, u32[]{:S(2)}, u32[]{:S(2)}) collective-permute-start(f32[16,72,128]{2,1,0:T(8,128)S(1)} %all_to_all.22.p_ref), channel_id=1, source_target_pairs={{0,1},{1,2},{2,3},{3,0},{4,7},{5,4},{6,5},{7,6},{8,9},{9,10},{10,1... | collective-permute-start | bytes 1769480 | tf_op jit(solution)/shard_map/ppermute | solution.py:275
  47.4 5.1 %copy-start.1 = (bf16[128,4096]{1,0:T(8,128)(2,1)S(1)}, bf16[128,4096]{1,0:T(8,128)(2,1)}, u32[]{:S(2)}) copy-start(bf16[128,4096]{1,0:T(8,128)(2,1)} %get-tuple-element.38.kt_ref) | copy-start | bytes 3145732
  52.2 5.1 %copy-start = (bf16[128,4096]{1,0:T(8,128)(2,1)S(1)}, bf16[128,4096]{1,0:T(8,128)(2,1)}, u32[]{:S(2)}) copy-start(bf16[128,4096]{1,0:T(8,128)(2,1)} %get-tuple-element.37.kt_ref) | copy-start | bytes 3145732
  52.2 5.1 %collective-permute-start.2 = (f32[16,72,128]{2,1,0:T(8,128)S(1)}, f32[16,72,128]{2,1,0:T(8,128)S(1)}, u32[]{:S(2)}, u32[]{:S(2)}) collective-permute-start(f32[16,72,128]{2,1,0:T(8,128)S(1)} %collective-permute-done.p_ref), channel_id=1, source_target_pairs={{0,4},{4,0},{1,5},{5,1},{2,6},{6,2},{3,7},{7,3},{8,12},{12,8},{9,1... | collective-permute-start | bytes 1769480 | tf_op jit(solution)/shard_map/ppermute | solution.py:301
  62.7 14.2 %all-to-all-start.2 = ((f32[128,1,128]{2,1,0:T(1,128)}), f32[128,1,128]{2,1,0:T(1,128)S(1)}, u32[]{:S(2)}, u32[]{:S(2)}) async-start(f32[128,1,128]{2,1,0:T(1,128)} %bitcast.2), calls=%async_computation.2 | async-start | bytes 131072 | tf_op jit(solution)/shard_map/all_to_all | solution.py:303
